TPU v7x, 512 devices: a whole 4x4x16 slice. The times are simulated.
512 devices in a mesh: gx: 16 (over x, y), gy: 16 (over z), ens: 2 (over core).
Axes of the slice: x: 4, y: 4, z: 16, core: 2. Of those that a mesh axis runs over, the one named last changes fastest.
Arguments:
- concentration: float32 [2, 4, 512, 2048], P('ens', None, 'gx', 'gy'), may hold values from 0 to 2
- cotangent: float32 [2, 4, 512, 2048], P('ens', None, 'gx', 'gy'), may hold values from -6 to 6
- vel_x: float32 [512, 2048], P('gx', 'gy'), may hold values from -2 to 2
- vel_y: float32 [512, 2048], P('gx', 'gy'), may hold values from -2 to 2
- dispersion: float32 [512, 2048], P('gx', 'gy'), may hold values from 1 to 10000
- wet_cells: int32 [512, 2048], P('gx', 'gy'), may hold values from 0 to 1
- decay_rate: float32 [4], replicated, may hold values from 0.05 to 1
- emission: float32 [4, 8192], replicated, may hold values from 2 to 40
- source_cell: int32 [8192], replicated, may hold values from 0 to 1048575
Outputs:
- state_next: float32 [2, 4, 512, 2048], P('ens', None, 'gx', 'gy')
- adjoint_state: float32 [2, 4, 512, 2048], P('ens', None, 'gx', 'gy')
- emission_grad: float32 [4, 8192], replicated
Inputs may be any that keep to these rules, and one draw needn't show every extreme that they name: `source_cell`: flat cell index, row * 2048 + column; several sources may share a cell.
All inputs are finite; a program needn't handle non-finite values.
Results may differ from a plain program's by a relative error of at most 0.0003.
Values sent between devices are 32-bit elements; how exact they have to be, the bound alone decides.
A program may use at most 64 MiB of HBM per device.

v0:
```python
import jax
import jax.numpy as jnp
from jax import lax
from jax.sharding import PartitionSpec as P


def with_halo(value, sides, width):
    for axis, dim in sides:
        size, length = (lax.axis_size(axis), value.shape[dim])
        up = [(i, (i + 1) % size) for i in range(size - 1)]
        down = [(j, i) for i, j in up]
        last = lax.slice_in_dim(value, length - width, length, axis=dim)
        first = lax.slice_in_dim(value, 0, width, axis=dim)
        before = lax.ppermute(last, axis, up)
        after = lax.ppermute(first, axis, down)
        value = jnp.concatenate([before, value, after], axis=dim)
    return value


def shift_line(values, stride, line_axis, fill_value):
    line_axis = line_axis % values.ndim
    length = values.shape[line_axis]
    pad_shape = list(values.shape)
    pad_shape[line_axis] = abs(stride)
    padding = jnp.full(pad_shape, fill_value, values.dtype)
    if stride > 0:
        kept_part = lax.slice_in_dim(values, 0, length - stride, axis=line_axis)
        return jnp.concatenate([padding, kept_part], axis=line_axis)
    kept_part = lax.slice_in_dim(values, -stride, length, axis=line_axis)
    return jnp.concatenate([kept_part, padding], axis=line_axis)


def cyclic_reduce(below_band, center_band, above_band, right_side, line_axis):
    length = right_side.shape[line_axis]
    stride = 1
    while stride < length:
        factor_before = -below_band / shift_line(center_band, stride, line_axis, 1.0)
        factor_after = -above_band / shift_line(center_band, -stride, line_axis, 1.0)
        new_center = (
            center_band
            + factor_before * shift_line(above_band, stride, line_axis, 0.0)
            + factor_after * shift_line(below_band, -stride, line_axis, 0.0)
        )
        right_side = (
            right_side
            + factor_before * shift_line(right_side, stride, line_axis, 0.0)
            + factor_after * shift_line(right_side, -stride, line_axis, 0.0)
        )
        below_band = factor_before * shift_line(below_band, stride, line_axis, 0.0)
        above_band = factor_after * shift_line(above_band, -stride, line_axis, 0.0)
        center_band = new_center
        stride = stride * 2
    return right_side / center_band


def tracer_copies(band, shape_like):
    return jnp.broadcast_to(band[None], shape_like.shape)


def band_pairs(
    velocity,
    disp_here,
    wet_here,
    vel_before,
    vel_after,
    disp_before,
    disp_after,
    wet_before,
    wet_after,
    decay_rate,
):
    open_before = wet_here * wet_before
    open_after = wet_here * wet_after
    flux_before = 0.5 * (disp_here + disp_before) * open_before
    flux_after = 0.5 * (disp_here + disp_after) * open_after
    inflow = jnp.maximum(velocity, 0.0)
    outflow = jnp.maximum(-velocity, 0.0)
    diagonal_base = 1.0 + flux_before + flux_after + inflow * open_before + outflow * open_after
    center = diagonal_base[None] + 0.5 * decay_rate[:, None, None]
    fwd_below = -(flux_before + inflow * open_before)
    fwd_above = -(flux_after + outflow * open_after)
    adj_below = -(flux_before + jnp.maximum(-vel_before, 0.0) * open_before)
    adj_above = -(flux_after + jnp.maximum(vel_after, 0.0) * open_after)
    forward = (tracer_copies(fwd_below, center), center, tracer_copies(fwd_above, center))
    adjoint = (tracer_copies(adj_below, center), center, tracer_copies(adj_above, center))
    return (forward, adjoint)


def single_system(bands):
    return tuple((band[None] for band in bands))


def take_row(values, row_index, line_axis):
    return lax.index_in_dim(values, row_index, axis=values.ndim + line_axis, keepdims=False)


def interface_solve(gathered, members):
    side_local = gathered[:, :, :members]
    first_part = gathered[:, :, members : 2 * members]
    coef_below = gathered[:, :, 2 * members]
    center_local = gathered[:, :, 2 * members + 1]
    end_above = gathered[:, :, 2 * members + 2]
    first_before = gathered[:, :, 2 * members + 3]
    first_after = gathered[:, :, 2 * members + 4]
    coef_center = center_local + end_above * shift_line(first_before, -1, 0, 0.0)
    coef_above = end_above * shift_line(first_after, -1, 0, 0.0)
    side_terms = side_local - end_above[:, :, None] * shift_line(first_part, -1, 0, 0.0)
    return cyclic_reduce(
        coef_below[:, :, None], coef_center[:, :, None], coef_above[:, :, None], side_terms, 0
    )


def couple_x(pieces, members):
    gathered = lax.all_gather(pieces[None], "gx", axis=0, tiled=True)
    solution = interface_solve(gathered, members)
    own_index = lax.axis_index("gx")
    own_value = lax.dynamic_index_in_dim(solution, own_index, 0, keepdims=False)
    left_value = lax.dynamic_index_in_dim(
        solution, jnp.maximum(own_index - 1, 0), 0, keepdims=False
    )
    return (left_value, own_value)


def couple_y(pieces, members):
    gathered = lax.all_gather(pieces[None], "gy", axis=0, tiled=True)
    solution = interface_solve(gathered, members)
    own_index = lax.axis_index("gy")
    own_value = lax.dynamic_index_in_dim(solution, own_index, 0, keepdims=False)
    left_value = lax.dynamic_index_in_dim(
        solution, jnp.maximum(own_index - 1, 0), 0, keepdims=False
    )
    return (left_value, own_value)


def line_solve(field_in, bands, line_axis, couple):
    below_band, center_band, above_band = bands
    members = field_in.shape[1]
    length = field_in.shape[line_axis]
    position = lax.broadcasted_iota(jnp.int32, center_band.shape, center_band.ndim + line_axis)
    first_row = position == 0
    last_row = position == length - 1
    local_below = jnp.where(first_row | last_row, 0.0, below_band)
    local_above = jnp.where(last_row, 0.0, above_band)
    local_center = jnp.where(last_row, 1.0, center_band)
    start_term = jnp.where(first_row, -below_band, 0.0)
    end_term = jnp.where(last_row, 1.0, 0.0)
    right_side = jnp.concatenate(
        [jnp.where(last_row[:, None], 0.0, field_in), start_term[:, None], end_term[:, None]],
        axis=1,
    )
    solved = cyclic_reduce(
        local_below[:, None], local_center[:, None], local_above[:, None], right_side, line_axis
    )
    particular = solved[:, :members]
    from_before = solved[:, members]
    from_after = solved[:, members + 1]
    end_below = take_row(below_band, length - 1, line_axis)
    end_center = take_row(center_band, length - 1, line_axis)
    end_above = take_row(above_band, length - 1, line_axis)
    end_field = take_row(field_in, length - 1, line_axis)
    coef_below = end_below * take_row(from_before, length - 2, line_axis)
    center_local = end_center + end_below * take_row(from_after, length - 2, line_axis)
    side_local = end_field - end_below[:, None] * take_row(particular, length - 2, line_axis)
    small_terms = jnp.stack(
        [
            coef_below,
            center_local,
            end_above,
            take_row(from_before, 0, line_axis),
            take_row(from_after, 0, line_axis),
        ],
        axis=1,
    )
    pieces = jnp.concatenate([side_local, take_row(particular, 0, line_axis), small_terms], axis=1)
    left_value, own_value = couple(pieces, members)
    return (
        particular
        + from_before[:, None] * jnp.expand_dims(left_value, line_axis)
        + from_after[:, None] * jnp.expand_dims(own_value, line_axis)
    )


def per_device(
    concentration, cotangent, vel_x, vel_y, dispersion, wet_cells, decay_rate, emission, source_cell
):
    members, tracers, rows_here, cols_here = concentration.shape
    stacked = jnp.stack([vel_x, vel_y, dispersion, wet_cells.astype(jnp.float32)])
    padded = with_halo(stacked, (("gx", 1), ("gy", 2)), 1)
    centre = padded[:, 1:-1, 1:-1]
    forward_x, adjoint_x = band_pairs(
        centre[0],
        centre[2],
        centre[3],
        padded[0, :-2, 1:-1],
        padded[0, 2:, 1:-1],
        padded[2, :-2, 1:-1],
        padded[2, 2:, 1:-1],
        padded[3, :-2, 1:-1],
        padded[3, 2:, 1:-1],
        decay_rate,
    )
    forward_y, adjoint_y = band_pairs(
        centre[1],
        centre[2],
        centre[3],
        padded[1, 1:-1, :-2],
        padded[1, 1:-1, 2:],
        padded[2, 1:-1, :-2],
        padded[2, 1:-1, 2:],
        padded[3, 1:-1, :-2],
        padded[3, 1:-1, 2:],
        decay_rate,
    )
    cols_total = cols_here * lax.axis_size("gy")
    row_start = lax.axis_index("gx") * rows_here
    col_start = lax.axis_index("gy") * cols_here
    source_rows = source_cell // cols_total
    source_cols = source_cell % cols_total
    owned_here = (
        (source_rows >= row_start)
        & (source_rows < row_start + rows_here)
        & (source_cols >= col_start)
        & (source_cols < col_start + cols_here)
    )
    local_index = jnp.where(
        owned_here, (source_rows - row_start) * cols_here + (source_cols - col_start), 0
    )
    weights = jnp.where(owned_here[None], emission, 0.0)
    source = (
        jnp.zeros((tracers, rows_here * cols_here), jnp.float32)
        .at[:, local_index]
        .add(weights)
        .reshape(tracers, rows_here, cols_here)
    )
    start_field = concentration + source[None]
    half_step = line_solve(start_field[None], single_system(forward_x), -2, couple_x)[0]
    state_next = line_solve(half_step[None], single_system(forward_y), -1, couple_y)[0]
    middle = line_solve(cotangent[None], single_system(adjoint_y), -1, couple_y)[0]
    adjoint_state = line_solve(middle[None], single_system(adjoint_x), -2, couple_x)[0]
    flat_adjoint = adjoint_state.reshape(members, tracers, rows_here * cols_here)
    picked = jnp.sum(flat_adjoint[:, :, local_index], axis=0)
    picked = jnp.where(owned_here[None], picked, 0.0)
    gradient = lax.psum(picked, ("gx", "gy", "ens"))
    return (state_next, adjoint_state, gradient)


def solution(mesh):
    in_specs = (
        P("ens", None, "gx", "gy"),
        P("ens", None, "gx", "gy"),
        P("gx", "gy"),
        P("gx", "gy"),
        P("gx", "gy"),
        P("gx", "gy"),
        P(),
        P(),
        P(),
    )
    out_specs = (P("ens", None, "gx", "gy"), P("ens", None, "gx", "gy"), P())
    return jax.shard_map(
        per_device, mesh=mesh, in_specs=in_specs, out_specs=out_specs, check_vma=False
    )
```

profile of v0, /device:TPU:1, one launch (start us, length us, event | category | flops | bytes accessed | tf_op | source)
XLA Modules:
  0.0 755.0 jit_solution(560131960686366789)
XLA Ops:
  7.2 0.7 convert_bitcast_fusion
  7.9 0.8 pad_maximum_fusion.32
  8.7 1.3 collective-permute-start.1
  10.0 4.7 collective-permute-start
  14.7 0.7 broadcast_multiply_fusion
  15.4 0.8 broadcast_clamp_fusion
  16.2 1.0 select_bitcast_fusion.1
  17.3 2.7 copy.481
  19.9 57.5 %scatter_custom_fusion = f32[4,4096]{0,1:T(8,128)S(1)} fusion(s32[8192]{0:T(1024)S(1)} %get-tuple-element.22, f32[8192,4]{1,0:T(8,128)} %copy.481, f32[]{:T(128)} %constant.41.clone.1), kind=kCustom, calls=%fused_computation.3 | custom fusion | flops 32768 | bytes 66048 | tf_op jit(solution)/shard_map/scatter-add | solution.py:232
  77.4 0.6 copy.564
  78.5 1.3 collective-permute-start.3
  79.8 4.4 collective-permute-start.2
  84.7 1.1 collective-permute-done.2
  85.8 0.2 broadcast_select_fusion
  86.5 0.2 fusion.136
  87.0 0.2 multiply_add_fusion.9
  87.2 0.2 fusion.135
  87.7 0.2 multiply_add_fusion.29
  88.2 0.2 multiply_add_fusion.8
  88.4 0.2 fusion.134
  89.2 0.2 multiply_add_fusion.7
  89.4 0.2 fusion.133
  90.2 0.2 multiply_add_fusion.6
  90.4 0.2 fusion.132
  91.2 0.2 multiply_add_fusion.5
  91.3 0.2 fusion.131
  92.1 0.2 multiply_add_fusion.4
  92.3 0.2 fusion.130
  92.6 0.1 fusion.100
  93.0 0.2 add_divide_fusion.1
  93.4 0.2 slice_reduce_fusion
  93.7 0.2 slice_reduce_fusion.1
  94.9 30.8 %all-gather.2 = f32[16,7,4,32]{3,2,1,0:T(4,128)S(1)} all-gather(f32[1,7,4,32]{3,2,1,0:T(4,128)S(1)} %constant_dynamic-update-slice_fusion.14), channel_id=4, replica_groups=mesh['gx'=16,'gy'=16,'ens'=2] {'gy'}, dimensions={0}, use_global_device_ids=true | all-gather | bytes 60928 | tf_op jit(solution)/shard_map/all_gather | solution.py:125
  126.7 0.2 pad_multiply_fusion.7
  126.8 0.2 pad_multiply_fusion.6
  127.4 0.2 multiply_add_fusion.23
  127.6 0.2 multiply_add_fusion.3
  130.6 21.2 %all-gather = f32[16,7,4,128]{3,2,1,0:T(4,128)S(1)} all-gather(f32[1,7,4,128]{3,2,1,0:T(4,128)S(1)} %constant_dynamic-update-slice_fusion), channel_id=2, replica_groups=mesh['gx'=16,'gy'=16,'ens'=2] {'gx'}, dimensions={0}, use_global_device_ids=true | all-gather | bytes 243712 | tf_op jit(solution)/shard_map/all_gather | solution.py:114
  152.6 0.2 fusion.144
  152.8 0.2 multiply_add_fusion.15
  153.0 0.2 fusion.143
  153.6 0.2 multiply_add_fusion.14
  153.7 0.2 fusion.142
  154.5 0.2 multiply_add_fusion.13
  154.7 0.2 fusion.141
  155.5 0.2 multiply_add_fusion.12
  155.7 0.2 fusion.140
  156.5 0.2 multiply_add_fusion.11
  156.7 0.2 fusion.139
  157.3 0.1 multiply_add_fusion.30
  157.4 0.2 multiply_add_fusion.10
  157.6 0.2 fusion.138
  158.3 0.2 add_divide_fusion.2
  158.6 0.2 slice_reduce_fusion.2
  159.1 0.2 slice_reduce_fusion.3
  160.1 22.2 %all-gather.1 = f32[16,7,4,32]{3,2,1,0:T(4,128)S(1)} all-gather(f32[1,7,4,32]{3,2,1,0:T(4,128)S(1)} %constant_dynamic-update-slice_fusion.7), channel_id=3, replica_groups=mesh['gx'=16,'gy'=16,'ens'=2] {'gy'}, dimensions={0}, use_global_device_ids=true | all-gather | bytes 60928 | tf_op jit(solution)/shard_map/all_gather | solution.py:125
  183.3 16.5 %all-gather.3 = f32[16,7,4,128]{3,2,1,0:T(4,128)S(1)} all-gather(f32[1,7,4,128]{3,2,1,0:T(4,128)S(1)} %constant_dynamic-update-slice_fusion.21), channel_id=5, replica_groups=mesh['gx'=16,'gy'=16,'ens'=2] {'gx'}, dimensions={0}, use_global_device_ids=true | all-gather | bytes 243712 | tf_op jit(solution)/shard_map/all_gather | solution.py:114
  200.5 0.6 copy.561
  201.2 27.9 %gather_fusion = f32[8192,4]{1,0:T(8,128)} fusion(f32[4,4096]{0,1:T(8,128)S(1)} %copy.561, s32[8192]{0:T(1024)S(1)} %get-tuple-element.21), kind=kCustom, calls=%fused_computation | custom fusion | bytes 294912 | tf_op jit(solution)/shard_map/gather | solution.py:241
  229.0 7.4 select_bitcast_fusion
  236.7 0.6 copy.595
  237.3 0.6 copy.562
  237.9 506.7 %all-reduce.314.cloned.1.call-done = f32[4,8192]{0,1:T(8,128)} async-done(((f32[4,8192]{0,1:T(8,128)}), f32[4,8192]{0,1:T(8,128)}) %all-reduce.314.cloned.1.call-update) | async-done | bytes 131088 | tf_op jit(solution)/shard_map/psum | solution.py:243
  744.7 3.5 copy.563
  (355 shorter events, 15.9 us)
Async XLA Ops:
  7.2 737.5 %all-reduce.314.cloned.1.call-start = ((), (), s32[]{:S(2)}) async-start(), calls=%async_computation | async-start | bytes 8388608 | tf_op jit(solution)/shard_map/psum | solution.py:243
  8.7 69.7 %collective-permute-start.1 = (f32[4,1,128]{2,1,0:T(1,128)S(1)}, f32[4,1,128]{2,1,0:T(1,128)S(1)}, u32[]{:S(2)}, u32[]{:S(2)}) collective-permute-start(f32[4,1,128]{2,1,0:T(1,128)S(1)} %get-tuple-element.403), channel_id=1, source_target_pairs={{32,0},{64,32},{96,64},{128,96},{160,128},{192,160},{224,192},{256... | collective-permute-start | bytes 6152 | tf_op jit(solution)/shard_map/ppermute | solution.py:15
  10.0 68.4 %collective-permute-start = (f32[4,1,128]{2,1,0:T(1,128)S(1)}, f32[4,1,128]{2,1,0:T(1,128)S(1)}, u32[]{:S(2)}, u32[]{:S(2)}) collective-permute-start(f32[4,1,128]{2,1,0:T(1,128)S(1)} %get-tuple-element.402), channel_id=1, source_target_pairs={{0,32},{32,64},{64,96},{96,128},{128,160},{160,192},{192,224},{224... | collective-permute-start | bytes 6152 | tf_op jit(solution)/shard_map/ppermute | solution.py:14
  17.2 60.9 %copy-start.5 = (f32[1,4,32,128]{3,2,1,0:T(8,128)S(1)}, f32[1,4,32,128]{3,2,1,0:T(8,128)}, u32[]{:S(2)}) copy-start(f32[1,4,32,128]{3,2,1,0:T(8,128)} %param.9) | copy-start | bytes 196612
  17.2 60.9 %copy-start.4 = (f32[1,4,32,128]{3,2,1,0:T(8,128)S(1)}, f32[1,4,32,128]{3,2,1,0:T(8,128)}, u32[]{:S(2)}) copy-start(f32[1,4,32,128]{3,2,1,0:T(8,128)} %param.10) | copy-start | bytes 196612
  17.2 61.2 %copy-start = (f32[32,128]{1,0:T(8,128)S(1)}, f32[32,128]{1,0:T(8,128)}, u32[]{:S(2)}) copy-start(f32[32,128]{1,0:T(8,128)} %param.13) | copy-start | bytes 49156
  17.2 61.2 %copy-start.1 = (f32[32,128]{1,0:T(8,128)S(1)}, f32[32,128]{1,0:T(8,128)}, u32[]{:S(2)}) copy-start(f32[32,128]{1,0:T(8,128)} %param.11) | copy-start | bytes 49156
  17.2 61.2 %copy-start.2 = (f32[32,128]{1,0:T(8,128)S(1)}, f32[32,128]{1,0:T(8,128)}, u32[]{:S(2)}) copy-start(f32[32,128]{1,0:T(8,128)} %param.12) | copy-start | bytes 49156
  17.2 67.0 %copy-start.3 = (s32[32,128]{1,0:T(8,128)S(1)}, s32[32,128]{1,0:T(8,128)}, u32[]{:S(2)}) copy-start(s32[32,128]{1,0:T(8,128)} %param.14) | copy-start | bytes 49156
  78.5 6.0 collective-permute-start.3
  79.8 5.9 collective-permute-start.2
Sparse Core Ops, SparseCore 0:
  236.6 508.0 all-reduce.313
where the time goes:
time: 757 us; the launch traced here: 755 us
  waiting for transfers between devices  508 us (67%)
  blocking collectives  90.7 us (12%)
  other arithmetic  80.4 us (11%)
  local copies, waits for them, and re-layouts  47.9 us (6%)
  between operations  16.5 us (2%)
  starting transfers between devices  11.7 us (2%)
    psum x1, waiting for transfers between devices, per_device(): gradient = lax.psum(picked, ('gx', 'gy', 'ens'))  507 us
    scatter-add x1, other arithmetic, per_device(): source = jnp.zeros((tracers, rows_here * cols_here), jnp.float32).at[:, l...  57.5 us
    all_gather x2, blocking collectives, couple_y(): gathered = lax.all_gather(pieces[None], 'gy', axis=0, tiled=True)  53 us
    all_gather x2, blocking collectives, couple_x(): gathered = lax.all_gather(pieces[None], 'gx', axis=0, tiled=True)  37.7 us
    gather x1, local copies, waits for them, and re-layouts, per_device(): picked = jnp.sum(flat_adjoint[:, :, local_index], axis=0)  27.9 us
  transfers between devices with their start and end apart: 5, of which 2 were waited for; matrix products, arithmetic and copies ran while one was open for 9% of the time, Pallas kernels for 0%

commit v1 on v0

v1 whole, which is shorter than its diff:
```python
import functools

import jax
import jax.numpy as jnp
from jax import lax
from jax.experimental import pallas as pl
from jax.experimental.pallas import tpu as pltpu
from jax.sharding import PartitionSpec as P

MESH = pl.DeviceIdType.MESH
TR, ROWS, COLS, LANES, Q = 4, 32, 128, 128, 16
F32, BF16 = jnp.float32, jnp.bfloat16
TILES = 8


def rolled(x, shift):
    n = x.shape[0]
    shift = shift % n
    if shift == 0:
        return x
    if shift % 8 == 0:
        return jnp.concatenate([x[n - shift :], x[: n - shift]], axis=0)
    return pltpu.roll(x, shift, 0)


def pcr_factor(below, center, above, count, unit):
    steps, stride = [], 1
    while stride < count:
        k = stride * unit
        inverse = 1.0 / center
        alpha = -below * rolled(inverse, k)
        gamma = -above * rolled(inverse, -k)
        center = center + alpha * rolled(above, k) + gamma * rolled(below, -k)
        below, above = alpha * rolled(below, k), gamma * rolled(above, -k)
        steps.append((k, alpha, gamma))
        stride *= 2
    return steps, 1.0 / center


def pcr_apply(factors, side):
    steps, inverse = factors
    for k, alpha, gamma in steps:
        side = side + alpha * rolled(side, k) + gamma * rolled(side, -k)
    return side * inverse


class Line:
    def __init__(self, size):
        self.size = size
        sub = lax.broadcasted_iota(jnp.int32, (8, LANES), 0) % size
        self.first = sub == 0
        self.last = sub == size - 1

    def extended(self, cells, before, after):
        head = jnp.where(self.first, before, rolled(cells[-1], 1))
        tail = jnp.where(self.last, after, rolled(cells[0], -1))
        return [head] + cells + [tail]

    def bands(self, vel, disp, wet, half_decay, before, after):
        vel = self.extended(vel, before[0], after[0])
        disp = self.extended(disp, before[1], after[1])
        wet = self.extended(wet, before[2], after[2])
        gate = [wet[k] * wet[k + 1] for k in range(Q + 1)]
        flux = [0.5 * (disp[k] + disp[k + 1]) * gate[k] for k in range(Q + 1)]
        plus = [jnp.maximum(v, 0.0) for v in vel]
        minus = [jnp.maximum(-v, 0.0) for v in vel]
        fwd_below = [-(flux[q] + plus[q + 1] * gate[q]) for q in range(Q)]
        fwd_above = [-(flux[q + 1] + minus[q + 1] * gate[q + 1]) for q in range(Q)]
        adj_below = [-(flux[q] + minus[q] * gate[q]) for q in range(Q)]
        adj_above = [-(flux[q + 1] + plus[q + 2] * gate[q + 1]) for q in range(Q)]
        center = [
            (1.0 + flux[q] + flux[q + 1] + plus[q + 1] * gate[q] + minus[q + 1] * gate[q + 1])
            + half_decay
            for q in range(Q)
        ]
        inverse = [1.0 / center[0]]
        for q in range(1, Q - 1):
            pivot = center[q] - fwd_below[q] * fwd_above[q - 1] * inverse[q - 1]
            inverse.append(1.0 / pivot)
        forward = self.factor(fwd_below, center, fwd_above, inverse, adj_below[0])
        adjoint = self.factor(adj_below, center, adj_above, inverse, fwd_below[0])
        return forward, adjoint

    def factor(self, below, center, above, inverse, above_prev):
        e = Q - 1
        mult = [None] + [below[q] * inverse[q - 1] for q in range(1, e)]
        up = [above[q] * inverse[q] for q in range(e)]
        start = [-below[0]]
        for q in range(1, e):
            start.append(-mult[q] * start[q - 1])
        v, w = [None] * e, [None] * e
        v[e - 1] = start[e - 1] * inverse[e - 1]
        w[e - 1] = -up[e - 1]
        for q in range(e - 2, -1, -1):
            v[q] = start[q] * inverse[q] - up[q] * v[q + 1]
            w[q] = -up[q] * w[q + 1]
        zero = jnp.zeros((8, LANES), F32)
        coef = below[e] * v[e - 1]
        center_local = center[e] + below[e] * w[e - 1]
        reduced = pcr_factor(
            jnp.where(self.first | self.last, zero, coef),
            jnp.where(self.last, 1.0, center_local + above[e] * rolled(v[0], -1)),
            jnp.where(self.last, zero, above[e] * rolled(w[0], -1)),
            self.size,
            1,
        )
        outer_v = pcr_apply(reduced, jnp.where(self.first, -coef, zero))
        outer_w = pcr_apply(reduced, jnp.where(self.last, 1.0, zero))
        fa = dict(
            mult=mult, up=up, inverse=inverse, v=v, w=w, below_end=below[e], above_end=above[e],
            coef=coef, reduced=reduced, outer_v=outer_v, outer_w=outer_w, above_prev=above_prev,
        )
        fa["center_terms"] = jnp.where(
            self.last,
            center_local + coef * rolled(outer_w, 1),
            above_prev * (v[0] + w[0] * outer_v),
        )
        fa["side_coefs"] = jnp.where(
            self.last, coef * rolled(outer_v, 1), above_prev * (w[0] * outer_w)
        )
        return fa

    def local(self, fa, field):
        e = Q - 1
        g = [field[0]]
        for q in range(1, e):
            g.append(field[q] - fa["mult"][q] * g[q - 1])
        part = [None] * e
        part[e - 1] = g[e - 1] * fa["inverse"][e - 1]
        for q in range(e - 2, -1, -1):
            part[q] = g[q] * fa["inverse"][q] - fa["up"][q] * part[q + 1]
        own = field[e] - fa["below_end"] * part[e - 1]
        inner = jnp.where(self.last, 0.0, own - fa["above_end"] * rolled(part[0], -1))
        outer = pcr_apply(fa["reduced"], inner)
        message = jnp.where(
            self.last,
            own - fa["coef"] * rolled(outer, 1),
            fa["above_prev"] * (part[0] + fa["w"][0] * outer),
        )
        return part, outer, message

    def finish(self, fa, part, outer, left, own):
        ends = outer + fa["outer_v"] * left + fa["outer_w"] * own
        before = jnp.where(self.first, left, rolled(ends, 1))
        cells = [part[q] + fa["v"][q] * before + fa["w"][q] * ends for q in range(Q - 1)]
        return cells + [ends]


def split(n):
    inner = 1
    while inner * inner < n:
        inner *= 2
    return n // inner, inner


def kernel(
    nx, ny, ne, nsrc,
    decay, conc, cot, vel_x, vel_y, disp, wet_cells, emission, cells,
    state_out, adjoint_out, grad_out,
    f_vx, f_vy, f_disp, f_wet, f_conc, f_cot, f_emis, f_cells,
    vel_t, disp_t, wet_t, work, work_t, state_v, adjoint_v,
    halo_send, halo_recv, onehot, rows_v, cols_v,
    y_send, y_recv, x_send, x_recv, xb_send, xb_recv, yb_send, yb_recv, ends_x, ends_y,
    picked, rs_recv, r1_send, r1_recv, r2_send, r2_recv, total, grad_v,
    in_sem, out_sem, halo_ssem, halo_rsem, ssem, rsem,
):
    gx, gy, en = lax.axis_index("gx"), lax.axis_index("gy"), lax.axis_index("ens")
    group = nx * ne
    me = gx * ne + en
    chunk = nsrc // group

    loads = [
        pltpu.make_async_copy(src, dst, in_sem.at[i])
        for i, (src, dst) in enumerate(
            [
                (vel_x, f_vx), (vel_y, f_vy), (disp, f_disp), (wet_cells, f_wet),
                (cells, f_cells), (cot.at[0], f_cot), (emission, f_emis), (conc.at[0], f_conc),
            ]
        )
    ]
    for load in loads:
        load.start()

    barrier = pltpu.get_barrier_semaphore()

    def greet_plane(o, _):
        peer = lax.rem(me + o, group)
        pl.semaphore_signal(
            barrier, inc=1, device_id=(peer // ne, gy, lax.rem(peer, ne)), device_id_type=MESH
        )
        return 0

    def greet_line(o, _):
        pl.semaphore_signal(
            barrier, inc=1, device_id=(gx, lax.rem(gy + o, ny), en), device_id_type=MESH
        )
        return 0

    lax.fori_loop(1, group, greet_plane, 0)
    lax.fori_loop(1, ny, greet_line, 0)

    def strided(ref, q):
        return ref[pl.ds(q, 8, stride=Q), :]

    def column(ref):
        return [strided(ref, q) for q in range(Q)]

    def put(ref, cells_):
        for q in range(Q):
            ref[pl.ds(q, 8, stride=Q), :] = cells_[q]

    for i in range(4):
        loads[i].wait()
    wet_f = f_wet[...].astype(F32)
    for field, ref in ((f_vy[...], vel_t), (f_disp[...], disp_t), (wet_f, wet_t)):
        ref[...] = jnp.transpose(jnp.concatenate([field] * TR, axis=0))
    zero8 = jnp.zeros((8, LANES), F32)
    for i in range(4):
        halo_send[i] = zero8
    halo_send[0, 0:1, :] = f_vx[ROWS - 1 : ROWS, :]
    halo_send[0, 1:2, :] = f_disp[ROWS - 1 : ROWS, :]
    halo_send[0, 2:3, :] = wet_f[ROWS - 1 : ROWS, :]
    halo_send[1, 0:1, :] = f_vx[0:1, :]
    halo_send[1, 1:2, :] = f_disp[0:1, :]
    halo_send[1, 2:3, :] = wet_f[0:1, :]
    for i, ref in enumerate((vel_t, disp_t, wet_t)):
        halo_send[2, i : i + 1, :] = ref[COLS - 1 : COLS, :]
        halo_send[3, i : i + 1, :] = ref[0:1, :]
    ends_x[0:8, :] = zero8
    ends_y[0:8, :] = zero8

    pl.semaphore_wait(barrier, group - 1 + ny - 1)

    halos = []
    for i, device in enumerate(
        (
            (lax.rem(gx + 1, nx), gy, en),
            (lax.rem(gx + nx - 1, nx), gy, en),
            (gx, lax.rem(gy + 1, ny), en),
            (gx, lax.rem(gy + ny - 1, ny), en),
        )
    ):
        halos.append(
            pltpu.make_async_remote_copy(
                src_ref=halo_send.at[i], dst_ref=halo_recv.at[i],
                send_sem=halo_ssem.at[i], recv_sem=halo_rsem.at[i],
                device_id=device, device_id_type=MESH,
            )
        )
    halos[2].start()
    halos[3].start()
    halos[0].start()
    halos[1].start()

    def along_line(send, recv, slot):
        def go(o, _):
            pltpu.make_async_remote_copy(
                src_ref=send, dst_ref=recv.at[gy], send_sem=ssem.at[slot],
                recv_sem=rsem.at[slot],
                device_id=(gx, lax.rem(gy + o, ny), en), device_id_type=MESH,
            ).start()
            return 0

        lax.fori_loop(1, ny, go, 0)
        recv[gy] = send[...]

    def along_x(send, recv, slot):
        def go(o, _):
            pltpu.make_async_remote_copy(
                src_ref=send, dst_ref=recv.at[gx], send_sem=ssem.at[slot],
                recv_sem=rsem.at[slot],
                device_id=(lax.rem(gx + o, nx), gy, en), device_id_type=MESH,
            ).start()
            return 0

        lax.fori_loop(1, nx, go, 0)
        recv[gx] = send[...]

    def arrived(recv, count, slot):
        pltpu.make_async_copy(
            recv.at[pl.ds(0, count)], recv.at[pl.ds(0, count)], rsem.at[slot]
        ).wait()

    def sent(recv, count, slot):
        pltpu.make_async_copy(
            recv.at[pl.ds(0, count)], recv.at[pl.ds(0, count)], ssem.at[slot]
        ).wait()

    loads[4].wait()
    shift = (ny * COLS).bit_length() - 1
    source = f_cells[...]
    rows_v[...] = lax.shift_right_logical(source, shift) - gx * ROWS
    cols_v[...] = (source & (ny * COLS - 1)) - gy * COLS
    row_iota = lax.broadcasted_iota(jnp.int32, (ROWS, LANES), 0)
    col_iota = lax.broadcasted_iota(jnp.int32, (COLS, LANES), 0)
    steps = nsrc // LANES // TILES

    def hot_columns(step, _):
        base = pl.multiple_of(step * TILES, TILES)
        tile = cols_v[pl.ds(base, TILES), :]
        for i in range(TILES):
            hot = jnp.where(col_iota == tile[i : i + 1, :], 1.0, 0.0).astype(BF16)
            onehot[:, pl.ds(pl.multiple_of((base + i) * LANES, LANES), LANES)] = hot
        return 0

    lax.fori_loop(0, steps, hot_columns, 0)

    loads[5].wait()
    work_t[...] = jnp.transpose(f_cot[...].reshape(TR * ROWS, COLS))

    y_line, x_line = Line(8), Line(2)
    halos[2].wait_recv()
    halos[3].wait_recv()
    lane_tracer = lax.broadcasted_iota(jnp.int32, (8, LANES), 1) // ROWS
    sub_tracer = lax.broadcasted_iota(jnp.int32, (8, LANES), 0) // 2

    def half_decay(tracer):
        value = jnp.full((8, LANES), decay[TR - 1], F32)
        for t in range(TR - 1):
            value = jnp.where(tracer == t, decay[t], value)
        return 0.5 * value

    def halo(i, keep):
        block = jnp.where(keep, halo_recv[i], 0.0)
        return [block[k : k + 1, :] for k in range(3)]

    y_fwd, y_adj = y_line.bands(
        column(vel_t), column(disp_t), column(wet_t), half_decay(lane_tracer),
        halo(2, gy > 0), halo(3, gy < ny - 1),
    )
    y_part, y_outer, message = y_line.local(y_adj, column(work_t))
    y_send[...] = zero8
    for i, term in enumerate((message, y_adj["center_terms"], y_adj["side_coefs"])):
        y_send[2 * i : 2 * i + 1, :] = term[0:1, :]
        y_send[2 * i + 1 : 2 * i + 2, :] = term[7:8, :]
    along_line(y_send, y_recv, 0)

    loads[6].wait()
    loads[7].wait()

    def scatter(step, acc):
        base = pl.multiple_of(step * TILES, TILES)
        tile = rows_v[pl.ds(base, TILES), :]
        start = pl.multiple_of(base * LANES, TILES * LANES)
        values = f_emis[:, pl.ds(start, TILES * LANES)]
        high = values.astype(BF16).astype(F32)
        low = values - high
        left = []
        for i in range(TILES):
            mask = row_iota == tile[i : i + 1, :]
            part = slice(i * LANES, (i + 1) * LANES)
            left.append(
                jnp.concatenate(
                    [
                        jnp.where(mask, half[t : t + 1, part], 0.0).astype(BF16)
                        for half in (high, low)
                        for t in range(TR)
                    ],
                    axis=0,
                )
            )
        return acc + lax.dot_general(
            jnp.concatenate(left, axis=1),
            onehot[:, pl.ds(start, TILES * LANES)],
            (((1,), (1,)), ((), ())),
            preferred_element_type=F32,
        )

    placed = lax.fori_loop(0, steps, scatter, jnp.zeros((2 * TR * ROWS, COLS), F32))
    work[...] = f_conc[...].reshape(TR * ROWS, COLS) + (placed[: TR * ROWS] + placed[TR * ROWS :])

    halos[0].wait_recv()
    halos[1].wait_recv()

    def spread(ref, as_float):
        upper = x_line.first
        out = []
        for q in range(Q):
            value = jnp.where(upper, ref[q : q + 1, :], ref[q + Q : q + Q + 1, :])
            out.append(value.astype(F32) if as_float else value)
        return out

    x_fwd, x_adj = x_line.bands(
        spread(f_vx, False), spread(f_disp, False), spread(f_wet, True), half_decay(sub_tracer),
        halo(0, gx > 0), halo(1, gx < nx - 1),
    )
    fx_part, fx_outer, message = x_line.local(x_fwd, column(work))
    x_send[0:8, :] = message
    x_send[8:16, :] = x_fwd["center_terms"]
    x_send[16:24, :] = x_fwd["side_coefs"]
    along_x(x_send, x_recv, 1)

    def y_piece(ref, k):
        return jnp.concatenate([ref[d, k : k + 1, :] for d in range(ny)], axis=0)

    def y_ends(factors, side):
        ends_y[8 : 8 + ny, :] = pcr_apply(factors, side)
        left = ends_y[pl.ds(7 + gy, 1), :]
        own = ends_y[pl.ds(8 + gy, 1), :]
        return left, own

    arrived(y_recv, ny - 1, 0)
    y_center = y_piece(y_recv, 3) + rolled(y_piece(y_recv, 2), -1)
    y_below, y_above = y_piece(y_recv, 5), rolled(y_piece(y_recv, 4), -1)
    factors = pcr_factor(y_below, y_center, y_above, ny, 1)
    left, own = y_ends(factors, y_piece(y_recv, 1) - rolled(y_piece(y_recv, 0), -1))
    put(work_t, y_line.finish(y_adj, y_part, y_outer, left, own))
    work[...] = jnp.transpose(work_t[...])
    ax_part, ax_outer, message = x_line.local(x_adj, column(work))
    xb_send[...] = message
    along_x(xb_send, xb_recv, 2)

    def x_piece(ref, k):
        return jnp.concatenate([ref[d, 8 * k : 8 * k + 8, :] for d in range(nx)], axis=0)

    def from_next(value):
        later = rolled(value, -8)
        return jnp.concatenate(
            [rolled(later[8 * d : 8 * d + 8], 1) for d in range(nx)], axis=0
        )

    def x_ends(factors, side):
        ends_x[8 : 8 + 8 * nx, :] = pcr_apply(factors, side)
        out = []
        for start in (gx, gx + 1):
            block = ends_x[pl.ds(pl.multiple_of(8 * start, 8), 8), :]
            out.append(jnp.where(x_line.last, block, rolled(block, -1)))
        return out

    arrived(x_recv, nx - 1, 1)
    terms = x_piece(x_recv, 1)
    x_center = terms + from_next(terms)
    terms = x_piece(x_recv, 2)
    x_below, x_above = terms, from_next(terms)
    factors = pcr_factor(x_below, x_center, x_above, nx, 8)
    terms = x_piece(x_recv, 0)
    left, own = x_ends(factors, terms - from_next(terms))
    put(work, x_line.finish(x_fwd, fx_part, fx_outer, left, own))
    work_t[...] = jnp.transpose(work[...])
    y_part, y_outer, message = y_line.local(y_fwd, column(work_t))
    yb_send[...] = zero8
    yb_send[0:1, :] = message[0:1, :]
    yb_send[1:2, :] = message[7:8, :]
    along_line(yb_send, yb_recv, 3)

    x_factors = pcr_factor(rolled(x_above, 8), x_center, rolled(x_below, -8), nx, 8)
    arrived(xb_recv, nx - 1, 2)
    terms = x_piece(xb_recv, 0)
    left, own = x_ends(x_factors, terms - from_next(terms))
    put(adjoint_v, x_line.finish(x_adj, ax_part, ax_outer, left, own))
    adjoint_store = pltpu.make_async_copy(
        adjoint_v, adjoint_out, out_sem.at[0]
    )
    adjoint_store.start()

    values = adjoint_v[...]
    high = values.astype(BF16)
    low = (values - high.astype(F32)).astype(BF16)
    both = jnp.concatenate([high, low], axis=1)

    def pick(step, _):
        base = pl.multiple_of(step * TILES, TILES)
        tile = rows_v[pl.ds(base, TILES), :]
        start = pl.multiple_of(base * LANES, TILES * LANES)
        hot = onehot[:, pl.ds(start, TILES * LANES)]
        found = jnp.dot(both, jnp.concatenate([hot, hot], axis=0), preferred_element_type=F32)
        for i in range(TILES):
            mask = row_iota == tile[i : i + 1, :]
            part = found[:, i * LANES : (i + 1) * LANES]
            lines = [
                jnp.sum(
                    jnp.where(mask, part[t * ROWS : (t + 1) * ROWS], 0.0), axis=0, keepdims=True
                )
                for t in range(TR)
            ]
            picked[:, pl.ds(pl.multiple_of((base + i) * LANES, LANES), LANES)] = jnp.concatenate(
                lines, axis=0
            )
        return 0

    lax.fori_loop(0, steps, pick, 0)

    def own_part(ref, j):
        return ref.at[:, pl.ds(pl.multiple_of(j * chunk, chunk), chunk)]

    def reduce_out(o, _):
        peer = lax.rem(me + o, group)
        pltpu.make_async_remote_copy(
            src_ref=own_part(picked, peer), dst_ref=rs_recv.at[me],
            send_sem=ssem.at[4], recv_sem=rsem.at[4],
            device_id=(peer // ne, gy, lax.rem(peer, ne)), device_id_type=MESH,
        ).start()
        return 0

    lax.fori_loop(1, group, reduce_out, 0)
    rs_recv[me] = picked[:, pl.ds(pl.multiple_of(me * chunk, chunk), chunk)]

    arrived(yb_recv, ny - 1, 3)
    y_factors = pcr_factor(rolled(y_above, 1), y_center, rolled(y_below, -1), ny, 1)
    left, own = y_ends(y_factors, y_piece(yb_recv, 1) - rolled(y_piece(yb_recv, 0), -1))
    put(work_t, y_line.finish(y_fwd, y_part, y_outer, left, own))
    state_v[...] = jnp.transpose(work_t[...])
    state_store = pltpu.make_async_copy(state_v, state_out, out_sem.at[1])
    state_store.start()

    arrived(rs_recv, group - 1, 4)

    def summed(ref, n):
        value = ref[0]
        for i in range(1, n):
            value = value + ref[i]
        return value

    outer, inner = split(ny)
    r1_send[...] = summed(rs_recv, group)
    for k in range(1, outer):
        pltpu.make_async_remote_copy(
            src_ref=r1_send, dst_ref=r1_recv.at[gy // inner],
            send_sem=ssem.at[5], recv_sem=rsem.at[5],
            device_id=(gx, lax.rem(gy + k * inner, ny), en), device_id_type=MESH,
        ).start()
    r1_recv[gy // inner] = r1_send[...]
    if outer > 1:
        arrived(r1_recv, outer - 1, 5)
    r2_send[...] = summed(r1_recv, outer)
    place = lax.rem(gy, inner)
    for k in range(1, inner):
        pltpu.make_async_remote_copy(
            src_ref=r2_send, dst_ref=r2_recv.at[place],
            send_sem=ssem.at[6], recv_sem=rsem.at[6],
            device_id=(gx, gy - place + lax.rem(place + k, inner), en), device_id_type=MESH,
        ).start()
    r2_recv[place] = r2_send[...]
    arrived(r2_recv, inner - 1, 6)
    total[...] = summed(r2_recv, inner)

    def spread_out(o, _):
        peer = lax.rem(me + o, group)
        pltpu.make_async_remote_copy(
            src_ref=total, dst_ref=own_part(grad_v, me),
            send_sem=ssem.at[7], recv_sem=rsem.at[7],
            device_id=(peer // ne, gy, lax.rem(peer, ne)), device_id_type=MESH,
        ).start()
        return 0

    lax.fori_loop(1, group, spread_out, 0)
    grad_v[:, pl.ds(pl.multiple_of(me * chunk, chunk), chunk)] = total[...]

    for copy in halos:
        copy.wait_send()
    sent(y_recv, ny - 1, 0)
    sent(x_recv, nx - 1, 1)
    sent(xb_recv, nx - 1, 2)
    sent(yb_recv, ny - 1, 3)
    sent(rs_recv, group - 1, 4)
    if outer > 1:
        sent(r1_recv, outer - 1, 5)
    sent(r2_recv, inner - 1, 6)
    adjoint_store.wait()
    state_store.wait()
    rest = grad_v.at[:, pl.ds(0, (group - 1) * chunk)]
    pltpu.make_async_copy(rest, rest, rsem.at[7]).wait()
    grad_store = pltpu.make_async_copy(grad_v, grad_out, out_sem.at[2])
    grad_store.start()
    pltpu.make_async_copy(rest, rest, ssem.at[7]).wait()
    grad_store.wait()


def per_device(
    nx, ny, ne, concentration, cotangent, vel_x, vel_y, dispersion, wet_cells, decay_rate, emission,
    source_cell,
):
    nsrc = source_cell.shape[0]
    group = nx * ne
    chunk = nsrc // group
    outer, inner = split(ny)
    square = pltpu.VMEM((TR * ROWS, COLS), F32)
    block = pltpu.VMEM((ROWS, COLS), F32)

    def vmem(*shape, dtype=F32):
        return pltpu.VMEM(shape, dtype)

    scratch = [
        block, block, block, vmem(ROWS, COLS, dtype=jnp.int32),
        vmem(TR, ROWS, COLS), vmem(TR, ROWS, COLS), vmem(TR, nsrc),
        vmem(nsrc // LANES, LANES, dtype=jnp.int32),
        square, square, square, square, square, square, square,
        vmem(4, 8, LANES), vmem(4, 8, LANES), vmem(COLS, nsrc, dtype=BF16),
        vmem(nsrc // LANES, LANES, dtype=jnp.int32), vmem(nsrc // LANES, LANES, dtype=jnp.int32),
        vmem(8, LANES), vmem(ny, 8, LANES), vmem(24, LANES), vmem(nx, 24, LANES),
        vmem(8, LANES), vmem(nx, 8, LANES), vmem(8, LANES), vmem(ny, 8, LANES),
        vmem(8 + 8 * nx, LANES), vmem(8 + max(8, ny), LANES),
        vmem(TR, nsrc), vmem(group, TR, chunk),
        vmem(TR, chunk), vmem(outer, TR, chunk), vmem(TR, chunk), vmem(inner, TR, chunk),
        vmem(TR, chunk), vmem(TR, nsrc),
        pltpu.SemaphoreType.DMA((8,)), pltpu.SemaphoreType.DMA((3,)),
        pltpu.SemaphoreType.DMA((4,)), pltpu.SemaphoreType.DMA((4,)),
        pltpu.SemaphoreType.DMA((8,)), pltpu.SemaphoreType.DMA((8,)),
    ]
    hbm = pl.BlockSpec(memory_space=pl.ANY)
    state, adjoint, gradient = pl.pallas_call(
        functools.partial(kernel, nx, ny, ne, nsrc),
        out_shape=(
            jax.ShapeDtypeStruct((TR * ROWS, COLS), F32),
            jax.ShapeDtypeStruct((TR * ROWS, COLS), F32),
            jax.ShapeDtypeStruct(emission.shape, F32),
        ),
        in_specs=[pl.BlockSpec(memory_space=pltpu.SMEM)] + [hbm] * 8,
        out_specs=(hbm, hbm, hbm),
        scratch_shapes=scratch,
        compiler_params=pltpu.CompilerParams(
            collective_id=0, has_side_effects=True, vmem_limit_bytes=32 * 1024 * 1024
        ),
        name="adi_step",
    )(
        decay_rate, concentration, cotangent, vel_x, vel_y, dispersion, wet_cells, emission,
        source_cell.reshape(nsrc // LANES, LANES),
    )
    shape = concentration.shape
    return (state.reshape(shape), adjoint.reshape(shape), gradient)


def solution(mesh):
    nx, ny, ne = (mesh.shape[a] for a in ("gx", "gy", "ens"))
    field = P("ens", None, "gx", "gy")
    plane = P("gx", "gy")
    return jax.shard_map(
        functools.partial(per_device, nx, ny, ne),
        mesh=mesh,
        in_specs=(field, field, plane, plane, plane, plane, P(), P(), P()),
        out_specs=(field, field, P()),
        check_vma=False,
    )
```

time: 757 us -> 68.8 us (0.09)
  waiting for transfers between devices: 508 us -> 0 us
  blocking collectives: 90.7 us -> 0 us
  other arithmetic: 80.4 us -> 0 us
  Pallas kernels: 0 us -> 58.9 us
  local copies, waits for them, and re-layouts: 47.9 us -> 8.77 us
  between operations: 16.5 us -> 0.66 us
  starting transfers between devices: 11.7 us -> 0 us
    psum x1 -> x0, waiting for transfers between devices: 507 us -> none  [per_device(): gradient = lax.psum(picked, ('gx', 'gy', 'ens'))]
    all_gather x4 -> x0, blocking collectives: 90.7 us -> none  [the longest x2 53 us: couple_y(): gathered = lax.all_gather(pieces[None], 'gy', axis=0, tiled=True)]
    pallas_call x0 -> x1, Pallas kernels: none -> 58.9 us  [per_device(): pl.pallas_call(functools.partial(kernel, nx, ny, ne, nsrc), out_shape=(ja...]
    scatter-add x1 -> x0, other arithmetic: 57.5 us -> none  [per_device(): source = jnp.zeros((tracers, rows_here * cols_here), jnp.float32).at[:, l...]
    gather x1 -> x0, local copies, waits for them, and re-layouts: 27.9 us -> none  [per_device(): picked = jnp.sum(flat_adjoint[:, :, local_index], axis=0)]
    ppermute x4 -> x0, starting transfers between devices: 11.6 us -> none  [the longest x2 9.07 us: with_halo(): before = lax.ppermute(last, axis, up)]
    slice x185 -> x0, local copies, waits for them, and re-layouts: 10.6 us -> none  [the longest x99 5.7 us: shift_line(): kept_part = lax.slice_in_dim(values, 0, length - stride, axis=line_axis)]
    select_n x8 -> x0, other arithmetic: 8.71 us -> none  [the longest x1 7.44 us: per_device(): picked = jnp.where(owned_here[None], picked, 0.0)]
  transfers between devices with their start and end apart: 5 -> 0, of which waited for: 2 -> 0; matrix products, arithmetic and copies ran while one was open for 9% -> 0% of each run, Pallas kernels for 0% -> 0%
where the time goes in v1:
time: 68.8 us; the launch traced here: 68.3 us
  Pallas kernels  58.9 us (86%)
  local copies, waits for them, and re-layouts  8.77 us (13%)
    pallas_call x1, Pallas kernels, per_device(): pl.pallas_call(functools.partial(kernel, nx, ny, ne, nsrc), out_shape=(ja...  58.9 us
    unnamed x21, local copies, waits for them, and re-layouts  8.77 us

profile of v1, /device:TPU:1, one launch (start us, length us, event | category | flops | bytes accessed | tf_op | source)
XLA Modules:
  0.0 68.3 jit_solution(9058161805124511964)
XLA Ops:
  0.6 0.0 copy-start.8
  0.6 0.6 copy-done.8
  1.3 0.0 copy-start
  1.3 0.9 %copy-done = f32[4,8192]{1,0:T(4,128)S(1)} copy-done((f32[4,8192]{1,0:T(4,128)S(1)}, f32[4,8192]{1,0:T(4,128)}, u32[]{:S(2)}) %copy-start) | copy-done | bytes 131096
  2.2 0.0 copy-start.1
  2.2 0.8 %copy-done.1 = f32[1,4,32,128]{3,2,1,0:T(8,128)S(1)} copy-done((f32[1,4,32,128]{3,2,1,0:T(8,128)S(1)}, f32[1,4,32,128]{3,2,1,0:T(8,128)}, u32[]{:S(2)}) %copy-start.1) | copy-done | bytes 65560
  3.0 0.0 copy-start.2
  3.0 0.8 %copy-done.2 = f32[1,4,32,128]{3,2,1,0:T(8,128)S(1)} copy-done((f32[1,4,32,128]{3,2,1,0:T(8,128)S(1)}, f32[1,4,32,128]{3,2,1,0:T(8,128)}, u32[]{:S(2)}) %copy-start.2) | copy-done | bytes 65560
  3.9 0.0 copy-start.3
  3.9 0.8 %copy-done.3 = s32[8192]{0:T(1024)S(1)} copy-done((s32[8192]{0:T(1024)S(1)}, s32[8192]{0:T(1024)}, u32[]{:S(2)}) %copy-start.3) | copy-done | bytes 32792
  4.6 0.0 copy-start.4
  4.6 0.7 %copy-done.4 = f32[32,128]{1,0:T(8,128)S(1)} copy-done((f32[32,128]{1,0:T(8,128)S(1)}, f32[32,128]{1,0:T(8,128)}, u32[]{:S(2)}) %copy-start.4) | copy-done | bytes 16408
  5.4 0.0 copy-start.5
  5.4 0.7 %copy-done.5 = f32[32,128]{1,0:T(8,128)S(1)} copy-done((f32[32,128]{1,0:T(8,128)S(1)}, f32[32,128]{1,0:T(8,128)}, u32[]{:S(2)}) %copy-start.5) | copy-done | bytes 16408
  6.1 0.0 copy-start.6
  6.1 0.7 %copy-done.6 = f32[32,128]{1,0:T(8,128)S(1)} copy-done((f32[32,128]{1,0:T(8,128)S(1)}, f32[32,128]{1,0:T(8,128)}, u32[]{:S(2)}) %copy-start.6) | copy-done | bytes 16408
  6.8 0.0 copy-start.7
  6.8 0.7 %copy-done.7 = s32[32,128]{1,0:T(8,128)S(1)} copy-done((s32[32,128]{1,0:T(8,128)S(1)}, s32[32,128]{1,0:T(8,128)}, u32[]{:S(2)}) %copy-start.7) | copy-done | bytes 16408
  7.5 58.9 %adi_step.1 = (f32[128,128]{1,0:T(8,128)S(1)}, f32[128,128]{1,0:T(8,128)S(1)}, f32[4,8192]{1,0:T(4,128)S(1)}) custom-call(f32[4]{0:T(128)S(1)} %copy-done.8, f32[1,4,32,128]{3,2,1,0:T(8,128)S(1)} %copy-done.1, f32[1,4,32,128]{3,2,1,0:T(8,128)S(1)} %copy-done.2, f32[32,128]{1,0:T(8,128)S(1)} %copy-done.4, f32[32,128]{1,0:T(8,128)S(1)} %copy-done.5, ...), custom_call_target="tpu_custom_call" | custom-call | tf_op jit(solution)/shard_map/adi_step/pallas_call | solution.py:601
  66.4 0.6 copy.15
  67.0 0.6 copy.16
  67.7 0.7 copy.17
Async XLA Ops:
  0.6 0.7 copy-start.8
  1.3 0.9 %copy-start = (f32[4,8192]{1,0:T(4,128)S(1)}, f32[4,8192]{1,0:T(4,128)}, u32[]{:S(2)}) copy-start(f32[4,8192]{1,0:T(4,128)} %emission.1) | copy-start | bytes 393220
  2.2 0.8 %copy-start.1 = (f32[1,4,32,128]{3,2,1,0:T(8,128)S(1)}, f32[1,4,32,128]{3,2,1,0:T(8,128)}, u32[]{:S(2)}) copy-start(f32[1,4,32,128]{3,2,1,0:T(8,128)} %conc.1) | copy-start | bytes 196612
  3.0 0.8 %copy-start.2 = (f32[1,4,32,128]{3,2,1,0:T(8,128)S(1)}, f32[1,4,32,128]{3,2,1,0:T(8,128)}, u32[]{:S(2)}) copy-start(f32[1,4,32,128]{3,2,1,0:T(8,128)} %cot.1) | copy-start | bytes 196612
  3.9 0.8 %copy-start.3 = (s32[8192]{0:T(1024)S(1)}, s32[8192]{0:T(1024)}, u32[]{:S(2)}) copy-start(s32[8192]{0:T(1024)} %param.17) | copy-start | bytes 98308
  4.6 0.7 %copy-start.4 = (f32[32,128]{1,0:T(8,128)S(1)}, f32[32,128]{1,0:T(8,128)}, u32[]{:S(2)}) copy-start(f32[32,128]{1,0:T(8,128)} %vel_x.1) | copy-start | bytes 49156
  5.4 0.7 %copy-start.5 = (f32[32,128]{1,0:T(8,128)S(1)}, f32[32,128]{1,0:T(8,128)}, u32[]{:S(2)}) copy-start(f32[32,128]{1,0:T(8,128)} %vel_y.1) | copy-start | bytes 49156
  6.1 0.7 %copy-start.6 = (f32[32,128]{1,0:T(8,128)S(1)}, f32[32,128]{1,0:T(8,128)}, u32[]{:S(2)}) copy-start(f32[32,128]{1,0:T(8,128)} %disp.1) | copy-start | bytes 49156
  6.8 0.7 %copy-start.7 = (s32[32,128]{1,0:T(8,128)S(1)}, s32[32,128]{1,0:T(8,128)}, u32[]{:S(2)}) copy-start(s32[32,128]{1,0:T(8,128)} %wet_cells.1) | copy-start | bytes 49156

commit v2 on v1

v2 whole, which is shorter than its diff:
```python
import functools

import jax
import jax.numpy as jnp
from jax import lax
from jax.experimental import pallas as pl
from jax.experimental.pallas import tpu as pltpu
from jax.sharding import PartitionSpec as P

MESH = pl.DeviceIdType.MESH
TR, ROWS, COLS, LANES, Q = 4, 32, 128, 128, 16
CELLS = TR * ROWS
F32, BF16 = jnp.float32, jnp.bfloat16
TILES = 8


def rolled(x, shift):
    n = x.shape[0]
    shift = shift % n
    if shift == 0:
        return x
    if shift % 8 == 0:
        return jnp.concatenate([x[n - shift :], x[: n - shift]], axis=0)
    return pltpu.roll(x, shift, 0)


def wrapped(i, n):
    return i & (n - 1) if n & (n - 1) == 0 else lax.rem(i, n)


def farthest_first(n):
    return sorted(range(1, n), key=lambda o: (-min(o, n - o), o))


def pcr_factor(below, center, above, count, unit):
    steps, stride = [], 1
    while stride < count:
        k = stride * unit
        inverse = 1.0 / center
        alpha = -below * rolled(inverse, k)
        gamma = -above * rolled(inverse, -k)
        center = center + alpha * rolled(above, k) + gamma * rolled(below, -k)
        below, above = alpha * rolled(below, k), gamma * rolled(above, -k)
        steps.append((k, alpha, gamma))
        stride *= 2
    return steps, 1.0 / center


def pcr_apply(factors, side):
    steps, inverse = factors
    for k, alpha, gamma in steps:
        side = side + alpha * rolled(side, k) + gamma * rolled(side, -k)
    return side * inverse


class Line:
    def __init__(self, size):
        self.size = size
        sub = lax.broadcasted_iota(jnp.int32, (8, LANES), 0) % size
        self.first = sub == 0
        self.last = sub == size - 1

    def extended(self, cells):
        head = jnp.where(self.first, 0.0, rolled(cells[-1], 1))
        tail = jnp.where(self.last, 0.0, rolled(cells[0], -1))
        return [head] + cells + [tail]

    def bands(self, vel, disp, wet, half_decay):
        vel, disp, wet = (self.extended(cells) for cells in (vel, disp, wet))
        gate = [wet[k] * wet[k + 1] for k in range(Q + 1)]
        flux = [0.5 * (disp[k] + disp[k + 1]) * gate[k] for k in range(Q + 1)]
        plus = [jnp.maximum(v, 0.0) for v in vel]
        minus = [jnp.maximum(-v, 0.0) for v in vel]
        fwd_below = [-(flux[q] + plus[q + 1] * gate[q]) for q in range(Q)]
        fwd_above = [-(flux[q + 1] + minus[q + 1] * gate[q + 1]) for q in range(Q)]
        adj_below = [-(flux[q] + minus[q] * gate[q]) for q in range(Q)]
        adj_above = [-(flux[q + 1] + plus[q + 2] * gate[q + 1]) for q in range(Q)]
        center = [
            (1.0 + flux[q] + flux[q + 1] + plus[q + 1] * gate[q] + minus[q + 1] * gate[q + 1])
            + half_decay
            for q in range(Q)
        ]
        inverse = [1.0 / center[0]]
        for q in range(1, Q - 1):
            pivot = center[q] - fwd_below[q] * fwd_above[q - 1] * inverse[q - 1]
            inverse.append(1.0 / pivot)
        forward = self.factor(fwd_below, center, fwd_above, inverse)
        adjoint = self.factor(adj_below, center, adj_above, inverse)
        return forward, adjoint

    def factor(self, below, center, above, inverse):
        e = Q - 1
        fa = dict(inverse=inverse, below_end=below[e], above_end=above[e])
        fa["mult"] = mult = [None] + [below[q] * inverse[q - 1] for q in range(1, e)]
        fa["up"] = up = [above[q] * inverse[q] for q in range(e)]
        start = [-below[0]]
        for q in range(1, e):
            start.append(-mult[q] * start[q - 1])
        v, w = [None] * e, [None] * e
        v[e - 1] = start[e - 1] * inverse[e - 1]
        w[e - 1] = -up[e - 1]
        for q in range(e - 2, -1, -1):
            v[q] = start[q] * inverse[q] - up[q] * v[q + 1]
            w[q] = -up[q] * w[q + 1]
        fa["v"], fa["w"] = v, w
        fa["reduced"] = pcr_factor(
            below[e] * v[e - 1],
            center[e] + below[e] * w[e - 1] + above[e] * rolled(v[0], -1),
            above[e] * rolled(w[0], -1),
            self.size,
            1,
        )
        head = jnp.where(self.first, 1.0, 0.0)
        fa["from_first"] = self.solve(fa, [head] + [None] * e)
        fa["from_last"] = self.solve(fa, [None] * e + [jnp.where(self.last, 1.0, 0.0)])
        return fa

    def solve(self, fa, field):
        def plus(a, b):
            return b if a is None else a if b is None else a + b

        def times(a, b):
            return None if b is None else a * b

        e = Q - 1
        g = [field[0]]
        for q in range(1, e):
            g.append(plus(field[q], times(-fa["mult"][q], g[q - 1])))
        part = [None] * e
        part[e - 1] = times(fa["inverse"][e - 1], g[e - 1])
        for q in range(e - 2, -1, -1):
            part[q] = plus(times(fa["inverse"][q], g[q]), times(-fa["up"][q], part[q + 1]))
        side = plus(field[e], times(-fa["below_end"], part[e - 1]))
        if part[0] is not None:
            side = side - fa["above_end"] * rolled(part[0], -1)
        ends = pcr_apply(fa["reduced"], side)
        before = rolled(ends, 1)
        return [
            plus(part[q], fa["v"][q] * before + fa["w"][q] * ends) for q in range(e)
        ] + [ends]

    def finish(self, fa, part, head, tail):
        first, last = fa["from_first"], fa["from_last"]
        return [part[q] + first[q] * head + last[q] * tail for q in range(Q)]

    def edges(self, cells):
        return jnp.where(self.last, cells[Q - 1], cells[0])


def faces(plus_first, disp_first, minus_last, disp_last, index, count):
    disp_next = rolled(disp_first, -1)
    shut = (index == count - 1) | (disp_last <= 0.0) | (disp_next <= 0.0)
    flux = 0.5 * (disp_last + disp_next)
    return (
        jnp.where(shut, 0.0, flux + minus_last),
        jnp.where(shut, 0.0, flux + rolled(plus_first, -1)),
    )


def kernel(
    nx, ny, ne, nsrc,
    decay, conc, cot, vel_x, vel_y, disp, wet_cells, emission, cells,
    state_out, adjoint_out, grad_out,
    f_vx, f_vy, f_disp, f_wet, f_conc, f_cot, f_emis, f_cells,
    vel_t, disp_t, wet_t, work, work_t, state_v, adjoint_v, mate_v, first_v, last_v,
    onehot, rows_v, cols_v, owner_v,
    y_send, y_recv, x_send, x_recv, xb_send, xb_recv, yb_send, yb_recv, ends_a, ends_b,
    z_send, z_recv, p_send, p_recv, g_send, g_recv, total, grad_v,
    in_sem, out_sem, mate_ssem, mate_rsem, ssem, rsem,
):
    gx, gy, en = lax.axis_index("gx"), lax.axis_index("gy"), lax.axis_index("ens")
    half = nsrc // ne
    chunk = half // nx
    tiles = chunk // LANES
    half_tiles = half // LANES
    mate = (gx, gy, wrapped(en + 1, ne))

    loads = [
        pltpu.make_async_copy(src, dst, in_sem.at[i])
        for i, (src, dst) in enumerate(
            [
                (vel_y, f_vy), (disp, f_disp), (wet_cells, f_wet), (cot.at[0], f_cot),
                (vel_x, f_vx), (cells, f_cells), (emission, f_emis), (conc.at[0], f_conc),
            ]
        )
    ]

    def line_peer(o):
        return (gx, wrapped(gy + o, ny), en)

    def x_peer(o):
        return (wrapped(gx + o, nx), gy, en)

    barrier = pltpu.get_barrier_semaphore()
    for o in farthest_first(ny):
        pl.semaphore_signal(barrier, inc=1, device_id=line_peer(o), device_id_type=MESH)
    for load in loads:
        load.start()
    for o in farthest_first(nx):
        pl.semaphore_signal(barrier, inc=1, device_id=x_peer(o), device_id_type=MESH)
    pl.semaphore_signal(barrier, inc=1, device_id=mate, device_id_type=MESH)

    def to_line(send, recv, slot):
        for o in farthest_first(ny):
            pltpu.make_async_remote_copy(
                src_ref=send, dst_ref=recv.at[gy], send_sem=ssem.at[slot],
                recv_sem=rsem.at[slot], device_id=line_peer(o), device_id_type=MESH,
            ).start()
        recv[gy] = send[...]

    def to_x(send, recv, slot):
        for o in farthest_first(nx):
            pltpu.make_async_remote_copy(
                src_ref=send, dst_ref=recv.at[gx], send_sem=ssem.at[slot],
                recv_sem=rsem.at[slot], device_id=x_peer(o), device_id_type=MESH,
            ).start()
        recv[gx] = send[...]

    def to_each_x(send, recv, slot):
        for o in farthest_first(nx):
            peer = wrapped(gx + o, nx)
            pltpu.make_async_remote_copy(
                src_ref=send.at[peer], dst_ref=recv.at[gx], send_sem=ssem.at[slot],
                recv_sem=rsem.at[slot], device_id=x_peer(o), device_id_type=MESH,
            ).start()
        recv[gx] = send[gx]

    def arrived(recv, count, slot):
        part = recv.at[pl.ds(0, count)]
        pltpu.make_async_copy(part, part, rsem.at[slot]).wait()

    def sent(recv, count, slot):
        part = recv.at[pl.ds(0, count)]
        pltpu.make_async_copy(part, part, ssem.at[slot]).wait()

    def strided(ref, q):
        return ref[pl.ds(q, 8, stride=Q), :]

    def column(ref):
        return [strided(ref, q) for q in range(Q)]

    def put(ref, cells_):
        for q in range(Q):
            ref[pl.ds(q, 8, stride=Q), :] = cells_[q]

    y_line, x_line = Line(8), Line(2)
    zero8 = jnp.zeros((8, LANES), F32)
    lane_tracer = lax.broadcasted_iota(jnp.int32, (8, LANES), 1) // ROWS
    sub_tracer = lax.broadcasted_iota(jnp.int32, (8, LANES), 0) // 2

    def half_decay(tracer):
        value = jnp.full((8, LANES), decay[TR - 1], F32)
        for t in range(TR - 1):
            value = jnp.where(tracer == t, decay[t], value)
        return 0.5 * value

    for i in range(4):
        loads[i].wait()
    wet_f = f_wet[...].astype(F32)
    for field, ref in ((f_vy[...], vel_t), (f_disp[...], disp_t), (wet_f, wet_t)):
        ref[...] = jnp.transpose(jnp.concatenate([field] * TR, axis=0))
    work_t[...] = jnp.transpose(f_cot[...].reshape(CELLS, COLS))
    y_fwd, y_adj = y_line.bands(
        column(vel_t), column(disp_t), column(wet_t), half_decay(lane_tracer)
    )
    y_part = y_line.solve(y_adj, column(work_t))
    end = COLS - 1
    tracer_row = lane_tracer[0:1]
    packed = jnp.where(
        tracer_row == 0,
        jnp.maximum(vel_t[0:1, :], 0.0),
        jnp.where(
            tracer_row == 1,
            disp_t[0:1, :] * wet_t[0:1, :],
            jnp.where(
                tracer_row == 2,
                jnp.maximum(-vel_t[end : end + 1, :], 0.0),
                disp_t[end : end + 1, :] * wet_t[end : end + 1, :],
            ),
        ),
    )
    e = Q - 1
    for i, row in enumerate(
        (
            y_part[0][0:1], y_part[e][7:8], y_fwd["from_first"][0][0:1],
            y_fwd["from_last"][e][7:8], y_fwd["from_last"][0][0:1],
            y_fwd["from_first"][e][7:8], packed, zero8[0:1],
        )
    ):
        y_send[i : i + 1, :] = row

    loads[4].wait()

    def spread(ref, as_float):
        out = []
        for q in range(Q):
            value = jnp.where(x_line.first, ref[q : q + 1, :], ref[q + Q : q + Q + 1, :])
            out.append(value.astype(F32) if as_float else value)
        return out

    x_fwd, x_adj = x_line.bands(
        spread(f_vx, False), spread(f_disp, False), spread(f_wet, True), half_decay(sub_tracer)
    )
    put(first_v, x_adj["from_first"])
    put(last_v, x_adj["from_last"])

    loads[5].wait()
    shift = (ny * COLS).bit_length() - 1
    source = f_cells[...]
    row = lax.shift_right_logical(source, shift)
    owner_v[...] = lax.shift_right_logical(row, ROWS.bit_length() - 1)
    rows_v[...] = row - gx * ROWS
    cols_v[...] = (source & (ny * COLS - 1)) - gy * COLS
    row_iota = lax.broadcasted_iota(jnp.int32, (ROWS, LANES), 0)
    col_iota = lax.broadcasted_iota(jnp.int32, (COLS, LANES), 0)

    def lanes(tile, count):
        return pl.ds(pl.multiple_of(tile * LANES, LANES), count * LANES)

    loads[6].wait()

    def scatter(step, acc):
        base = pl.multiple_of(step * TILES, TILES)
        row_tile = rows_v[pl.ds(base, TILES), :]
        col_tile = cols_v[pl.ds(base, TILES), :]
        values = f_emis[:, lanes(base, TILES)]
        high = values.astype(BF16).astype(F32)
        low = values - high
        left, hots = [], []
        for i in range(TILES):
            mask = row_iota == row_tile[i : i + 1, :]
            part = slice(i * LANES, (i + 1) * LANES)
            left.append(
                jnp.concatenate(
                    [
                        jnp.where(mask, piece[t : t + 1, part], 0.0).astype(BF16)
                        for piece in (high, low)
                        for t in range(TR)
                    ],
                    axis=0,
                )
            )
            hots.append(jnp.where(col_iota == col_tile[i : i + 1, :], 1.0, 0.0).astype(BF16))
        hot = jnp.concatenate(hots, axis=1)
        onehot[:, lanes(base, TILES)] = hot
        return acc + lax.dot_general(
            jnp.concatenate(left, axis=1),
            hot,
            (((1,), (1,)), ((), ())),
            preferred_element_type=F32,
        )

    placed = lax.fori_loop(
        0, nsrc // LANES // TILES, scatter, jnp.zeros((2 * CELLS, COLS), F32)
    )
    loads[7].wait()
    work[...] = f_conc[...].reshape(CELLS, COLS) + (placed[:CELLS] + placed[CELLS:])
    fx_part = x_line.solve(x_fwd, column(work))
    x_send[0:8, :] = x_line.edges(fx_part)
    x_send[8:16, :] = jnp.where(x_line.last, x_fwd["from_last"][e], x_fwd["from_first"][0])
    x_send[16:24, :] = jnp.where(x_line.last, x_fwd["from_first"][e], x_fwd["from_last"][0])
    x_send[24:25, :] = jnp.maximum(f_vx[0:1, :], 0.0)
    x_send[25:26, :] = f_disp[0:1, :] * wet_f[0:1, :]
    x_send[26:27, :] = jnp.maximum(-f_vx[ROWS - 1 : ROWS, :], 0.0)
    x_send[27:28, :] = f_disp[ROWS - 1 : ROWS, :] * wet_f[ROWS - 1 : ROWS, :]
    x_send[28:32, :] = zero8[0:4]
    ends_a[0:8, :] = zero8
    ends_b[0:8, :] = zero8

    pl.semaphore_wait(barrier, ny - 1 + nx - 1 + 1)
    to_line(y_send, y_recv, 0)
    to_x(x_send, x_recv, 1)

    def split_bf16(values):
        high = values.astype(BF16)
        return jnp.concatenate([high, (values - high.astype(F32)).astype(BF16)], axis=1)

    def pick(fields, send, at):
        left = jnp.concatenate([split_bf16(field) for field in fields], axis=0)
        per_step = max(TILES, tiles)

        def go(step, _):
            base = pl.multiple_of(en * half_tiles + step * per_step, per_step)
            row_tile = rows_v[pl.ds(base, per_step), :]
            hot = onehot[:, lanes(base, per_step)]
            found = jnp.dot(left, jnp.concatenate([hot, hot], axis=0), preferred_element_type=F32)
            for i in range(per_step):
                mask = row_iota == row_tile[i : i + 1, :]
                block = step * (per_step // tiles) + i // tiles
                for k, first in enumerate(at):
                    for t in range(TR):
                        start = (k * TR + t) * ROWS
                        line = found[start : start + ROWS, i * LANES : (i + 1) * LANES]
                        line = jnp.sum(jnp.where(mask, line, 0.0), axis=0, keepdims=True)
                        spot = first + tiles * t + i % tiles
                        send[block, spot : spot + 1, :] = line
            return 0

        lax.fori_loop(0, half_tiles // per_step, go, 0)

    pick((first_v[...], last_v[...]), z_send, (0, TR * tiles))
    to_each_x(z_send, z_recv, 2)

    def x_piece(ref, k):
        return jnp.concatenate([ref[d, 8 * k : 8 * k + 8, :] for d in range(nx)], axis=0)

    def single(ref, k, n):
        return jnp.concatenate([ref[d, k : k + 1, :] for d in range(n)], axis=0)

    def expanded(rows):
        return jnp.concatenate(
            [jnp.broadcast_to(rows[d : d + 1], (8, LANES)) for d in range(nx)], axis=0
        )

    def from_next(value):
        later = rolled(value, -8)
        return jnp.concatenate([rolled(later[8 * d : 8 * d + 8], 1) for d in range(nx)], axis=0)

    def own_x(ref, at):
        block = ref[pl.ds(pl.multiple_of(8 * at, 8), 8), :]
        return jnp.where(x_line.last, block, rolled(block, -1))

    arrived(x_recv, nx - 1, 1)
    index = lax.broadcasted_iota(jnp.int32, (nx, LANES), 0)
    x_before, x_after = (
        expanded(face) for face in faces(*[single(x_recv, 24 + k, nx) for k in range(4)], index, nx)
    )
    diagonal, corner = x_piece(x_recv, 1), x_piece(x_recv, 2)
    x_below = -corner * rolled(x_after, 8)
    x_center = 1.0 + diagonal * x_before + from_next(diagonal) * x_after
    block_index = lax.broadcasted_iota(jnp.int32, (8 * nx, LANES), 0) // 8
    x_above = jnp.where(
        block_index == nx - 1, 0.0, -from_next(corner) * rolled(x_before, -8)
    )
    terms = x_piece(x_recv, 0)
    jump = pcr_apply(pcr_factor(x_below, x_center, x_above, nx, 8), terms - from_next(terms))
    ends_a[8 : 8 + 8 * nx, :] = x_after * jump
    ends_b[8 : 8 + 8 * nx, :] = x_before * jump
    put(work, x_line.finish(x_fwd, fx_part, own_x(ends_a, gx), -own_x(ends_b, gx + 1)))
    work_t[...] = jnp.transpose(work[...])
    fy_part = y_line.solve(y_fwd, column(work_t))
    yb_send[0:1, :] = fy_part[0][0:1]
    yb_send[1:2, :] = fy_part[e][7:8]
    yb_send[2:8, :] = zero8[0:6]
    to_line(yb_send, yb_recv, 3)
    x_factors = pcr_factor(rolled(x_above, 8), x_center, rolled(x_below, -8), nx, 8)

    arrived(y_recv, ny - 1, 0)
    raw = single(y_recv, 6, ny)
    tracer_n = jnp.broadcast_to(tracer_row, (ny, LANES))
    quantities = []
    for k in range(4):
        value = jnp.where(tracer_n == k, raw, 0.0)
        value = value + pltpu.roll(value, ROWS, 1)
        quantities.append(value + pltpu.roll(value, 2 * ROWS, 1))
    index = lax.broadcasted_iota(jnp.int32, (ny, LANES), 0)
    y_before, y_after = faces(*quantities, index, ny)
    g00, gnn, g0n, gn0 = (single(y_recv, k, ny) for k in (2, 3, 4, 5))
    y_below = -gn0 * rolled(y_after, 1)
    y_center = 1.0 + gnn * y_before + rolled(g00, -1) * y_after
    y_above = jnp.where(index == ny - 1, 0.0, -rolled(g0n * y_before, -1))
    y_factors = pcr_factor(rolled(y_above, 1), y_center, rolled(y_below, -1), ny, 1)
    ends_a[8 : 8 + ny, :] = pcr_apply(
        y_factors, y_before * single(y_recv, 1, ny) - y_after * rolled(single(y_recv, 0, ny), -1)
    )
    head, tail = ends_a[pl.ds(7 + gy, 1), :], -ends_a[pl.ds(8 + gy, 1), :]
    put(work_t, y_line.finish(y_adj, y_part, head, tail))
    work[...] = jnp.transpose(work_t[...])
    ax_part = x_line.solve(x_adj, column(work))
    put(adjoint_v, ax_part)
    to_mate = pltpu.make_async_remote_copy(
        src_ref=adjoint_v, dst_ref=mate_v, send_sem=mate_ssem.at[0], recv_sem=mate_rsem.at[0],
        device_id=mate, device_id_type=MESH,
    )
    to_mate.start()
    xb_send[...] = x_line.edges(ax_part)
    to_x(xb_send, xb_recv, 4)

    to_mate.wait_recv()
    both = adjoint_v[...] + mate_v[...]
    work[...] = both
    both_edges = x_line.edges([strided(work, q) if q in (0, e) else None for q in range(Q)])
    for d in range(nx):
        p_send[d, 0:8, :] = both_edges
    pick((both,), p_send, (8,))
    to_each_x(p_send, p_recv, 5)

    y_fwd_factors = pcr_factor(y_below, y_center, y_above, ny, 1)
    arrived(z_recv, nx - 1, 2)

    def summed(ref, first, count, n):
        value = ref[0, first : first + count, :]
        for i in range(1, n):
            value = value + ref[i, first : first + count, :]
        return value

    width = TR * tiles
    z_first, z_last = summed(z_recv, 0, width, nx), summed(z_recv, width, width, nx)

    arrived(p_recv, nx - 1, 5)

    def flux_of(ref):
        terms = x_piece(ref, 0)
        return pcr_apply(x_factors, x_before * terms - x_after * from_next(terms))

    flux = flux_of(p_recv)
    mine = pl.multiple_of(en * half_tiles + gx * tiles, tiles)
    hot = onehot[:, lanes(mine, tiles)]
    found = jnp.dot(
        split_bf16(flux), jnp.concatenate([hot, hot], axis=0), preferred_element_type=F32
    )
    owner = owner_v[pl.ds(mine, tiles), :]
    for i in range(tiles):
        into, out = zero8, zero8
        for d in range(nx):
            value = found[8 * d : 8 * d + 8, i * LANES : (i + 1) * LANES]
            into = into + jnp.where(owner[i : i + 1, :] == d + 1, value, 0.0)
            out = out + jnp.where(owner[i : i + 1, :] == d, value, 0.0)
        for t in range(TR):
            spot = slice(tiles * t + i, tiles * t + i + 1)
            at = slice(2 * t + 1, 2 * t + 2)
            g_send[spot, :] = z_first[spot] * into[at] - z_last[spot] * out[at]
    g_send[...] = g_send[...] + summed(p_recv, 8, width, nx)
    to_line(g_send, g_recv, 6)

    arrived(xb_recv, nx - 1, 4)
    ends_a[8 : 8 + 8 * nx, :] = flux_of(xb_recv)
    put(
        work,
        x_line.finish(x_adj, column(adjoint_v), own_x(ends_a, gx), -own_x(ends_a, gx + 1)),
    )
    adjoint_store = pltpu.make_async_copy(work, adjoint_out, out_sem.at[0])
    adjoint_store.start()

    arrived(yb_recv, ny - 1, 3)
    jump = pcr_apply(
        y_fwd_factors, single(yb_recv, 1, ny) - rolled(single(yb_recv, 0, ny), -1)
    )
    ends_a[8 : 8 + ny, :] = y_after * jump
    ends_b[8 : 8 + ny, :] = y_before * jump
    head, tail = ends_a[pl.ds(7 + gy, 1), :], -ends_b[pl.ds(8 + gy, 1), :]
    put(work_t, y_line.finish(y_fwd, fy_part, head, tail))
    state_v[...] = jnp.transpose(work_t[...])
    state_store = pltpu.make_async_copy(state_v, state_out, out_sem.at[1])
    state_store.start()

    arrived(g_recv, ny - 1, 6)
    sums = summed(g_recv, 0, width, ny)
    for t in range(TR):
        for i in range(tiles):
            total[t : t + 1, i * LANES : (i + 1) * LANES] = sums[tiles * t + i : tiles * t + i + 1]

    def span(start, size):
        return grad_v.at[:, pl.ds(pl.multiple_of(start, LANES), size)]

    here = en * half + gx * chunk
    for o in farthest_first(nx):
        pltpu.make_async_remote_copy(
            src_ref=total, dst_ref=span(here, chunk), send_sem=ssem.at[7], recv_sem=rsem.at[7],
            device_id=x_peer(o), device_id_type=MESH,
        ).start()
    grad_v[:, pl.ds(pl.multiple_of(here, LANES), chunk)] = total[...]

    sent(y_recv, ny - 1, 0)
    sent(x_recv, nx - 1, 1)
    sent(z_recv, nx - 1, 2)
    sent(yb_recv, ny - 1, 3)
    sent(xb_recv, nx - 1, 4)
    sent(p_recv, nx - 1, 5)
    sent(g_recv, ny - 1, 6)
    to_mate.wait_send()
    adjoint_store.wait()
    state_store.wait()

    rest = span(0, (nx - 1) * chunk)
    pltpu.make_async_copy(rest, rest, rsem.at[7]).wait()
    own_half = span(en * half, half)
    swap = pltpu.make_async_remote_copy(
        src_ref=own_half, dst_ref=own_half, send_sem=mate_ssem.at[1], recv_sem=mate_rsem.at[1],
        device_id=mate, device_id_type=MESH,
    )
    swap.start()
    pltpu.make_async_copy(rest, rest, ssem.at[7]).wait()
    swap.wait()
    grad_store = pltpu.make_async_copy(grad_v, grad_out, out_sem.at[2])
    grad_store.start()
    grad_store.wait()


def per_device(
    nx, ny, ne, concentration, cotangent, vel_x, vel_y, dispersion, wet_cells, decay_rate, emission,
    source_cell,
):
    nsrc = source_cell.shape[0]
    chunk = nsrc // (nx * ne)
    width = TR * chunk // LANES
    square = pltpu.VMEM((CELLS, COLS), F32)
    block = pltpu.VMEM((ROWS, COLS), F32)

    def vmem(*shape, dtype=F32):
        return pltpu.VMEM(shape, dtype)

    index = vmem(nsrc // LANES, LANES, dtype=jnp.int32)
    ends = vmem(8 + 8 * max(nx, ny), LANES)
    scratch = [
        block, block, block, vmem(ROWS, COLS, dtype=jnp.int32),
        vmem(TR, ROWS, COLS), vmem(TR, ROWS, COLS), vmem(TR, nsrc), index,
        square, square, square, square, square, square, square, square, square, square,
        vmem(COLS, nsrc, dtype=BF16), index, index, index,
        vmem(8, LANES), vmem(ny, 8, LANES), vmem(32, LANES), vmem(nx, 32, LANES),
        vmem(8, LANES), vmem(nx, 8, LANES), vmem(8, LANES), vmem(ny, 8, LANES), ends, ends,
        vmem(nx, 2 * width, LANES), vmem(nx, 2 * width, LANES),
        vmem(nx, 8 + width, LANES), vmem(nx, 8 + width, LANES),
        vmem(width, LANES), vmem(ny, width, LANES), vmem(TR, chunk), vmem(TR, nsrc),
        pltpu.SemaphoreType.DMA((8,)), pltpu.SemaphoreType.DMA((3,)),
        pltpu.SemaphoreType.DMA((2,)), pltpu.SemaphoreType.DMA((2,)),
        pltpu.SemaphoreType.DMA((8,)), pltpu.SemaphoreType.DMA((8,)),
    ]
    hbm = pl.BlockSpec(memory_space=pl.ANY)
    state, adjoint, gradient = pl.pallas_call(
        functools.partial(kernel, nx, ny, ne, nsrc),
        out_shape=(
            jax.ShapeDtypeStruct((CELLS, COLS), F32),
            jax.ShapeDtypeStruct((CELLS, COLS), F32),
            jax.ShapeDtypeStruct(emission.shape, F32),
        ),
        in_specs=[pl.BlockSpec(memory_space=pltpu.SMEM)] + [hbm] * 8,
        out_specs=(hbm, hbm, hbm),
        scratch_shapes=scratch,
        compiler_params=pltpu.CompilerParams(
            collective_id=0, has_side_effects=True, vmem_limit_bytes=VMEM_BYTES
        ),
        name="adi_step",
    )(
        decay_rate, concentration, cotangent, vel_x, vel_y, dispersion, wet_cells, emission,
        source_cell.reshape(nsrc // LANES, LANES),
    )
    shape = concentration.shape
    return (state.reshape(shape), adjoint.reshape(shape), gradient)


VMEM_BYTES = 60 * 1024 * 1024


def solution(mesh):
    nx, ny, ne = (mesh.shape[a] for a in ("gx", "gy", "ens"))
    field = P("ens", None, "gx", "gy")
    plane = P("gx", "gy")
    return jax.shard_map(
        functools.partial(per_device, nx, ny, ne),
        mesh=mesh,
        in_specs=(field, field, plane, plane, plane, plane, P(), P(), P()),
        out_specs=(field, field, P()),
        check_vma=False,
    )
```

time: 68.8 us -> 50.1 us (0.73)
  Pallas kernels: 58.9 us -> 46.4 us
  local copies, waits for them, and re-layouts: 8.77 us -> 2.8 us
    pallas_call x1, Pallas kernels: 58.9 us -> 46.4 us  [per_device(): pl.pallas_call(functools.partial(kernel, nx, ny, ne, nsrc), out_shape=(ja...]
    unnamed x21 -> x7, local copies, waits for them, and re-layouts: 8.77 us -> 2.8 us
where the time goes in v2:
time: 50.1 us; the launch traced here: 49.9 us
  Pallas kernels  46.4 us (93%)
  local copies, waits for them, and re-layouts  2.8 us (6%)
  between operations  0.66 us (1%)
    pallas_call x1, Pallas kernels, per_device(): pl.pallas_call(functools.partial(kernel, nx, ny, ne, nsrc), out_shape=(ja...  46.4 us
    unnamed x7, local copies, waits for them, and re-layouts  2.8 us

profile of v2, /device:TPU:1, one launch (start us, length us, event | category | flops | bytes accessed | tf_op | source)
XLA Modules:
  0.0 49.9 jit_solution(718568389807253545)
XLA Ops:
  0.6 46.4 %adi_step.1 = (f32[128,128]{1,0:T(8,128)}, f32[128,128]{1,0:T(8,128)}, f32[4,8192]{1,0:T(4,128)}) custom-call(f32[4]{0:T(128)} %decay.1, f32[1,4,32,128]{3,2,1,0:T(8,128)} %conc.1, f32[1,4,32,128]{3,2,1,0:T(8,128)} %cot.1, f32[32,128]{1,0:T(8,128)} %vel_x.1, f32[32,128]{1,0:T(8,128)} %vel_y.1, f32[32,128]{1,0:T(8,128)} %disp.1, s32[32,128]{1,0:T(8,128)} %wet_cells.1, ...), custom_call_target="tpu_custom_call" | custom-call | tf_op jit(solution)/shard_map/adi_step/pallas_call | solution.py:620
  47.1 0.0 copy-start.1
  47.1 0.0 copy-start
  47.1 1.5 %copy.15 = f32[1,4,32,128]{3,2,1,0:T(8,128)} copy(f32[1,4,32,128]{3,2,1,0:T(8,128)} %bitcast.4) | data formatting | bytes 131072
  48.6 0.0 copy-done.1
  48.6 0.6 %copy.16 = f32[1,4,32,128]{3,2,1,0:T(8,128)} copy(f32[1,4,32,128]{3,2,1,0:T(8,128)S(1)} %bitcast.3) | data formatting | bytes 131072
  49.2 0.0 copy-done
  49.2 0.7 %copy.17 = f32[4,8192]{1,0:T(4,128)} copy(f32[4,8192]{1,0:T(4,128)S(1)} %copy-done) | data formatting | bytes 262144
Async XLA Ops:
  47.1 1.5 %copy-start.1 = (f32[128,128]{1,0:T(8,128)S(1)}, f32[128,128]{1,0:T(8,128)}, u32[]{:S(2)}) copy-start(f32[128,128]{1,0:T(8,128)} %get-tuple-element.7) | copy-start | bytes 196612
  47.1 2.2 %copy-start = (f32[4,8192]{1,0:T(4,128)S(1)}, f32[4,8192]{1,0:T(4,128)}, u32[]{:S(2)}) copy-start(f32[4,8192]{1,0:T(4,128)} %get-tuple-element.14) | copy-start | bytes 393220

commit v3 on v2

--- a/solution.py
+++ b/solution.py
@@ -30,6 +30,11 @@
 
 def farthest_first(n):
     return sorted(range(1, n), key=lambda o: (-min(o, n - o), o))
+
+
+def plane_order(n):
+    far = (0, 1, 2, 1)
+    return sorted(range(1, n), key=lambda o: -(far[o % 4] + far[o // 4 % 4]))
 
 
 def pcr_factor(below, center, above, count, unit):
@@ -159,14 +164,14 @@
 
 def kernel(
     nx, ny, ne, nsrc,
-    decay, conc, cot, vel_x, vel_y, disp, wet_cells, emission, cells,
+    decay_in, conc, cot, vel_x, vel_y, disp, wet_cells, emission, cells,
     state_out, adjoint_out, grad_out,
-    f_vx, f_vy, f_disp, f_wet, f_conc, f_cot, f_emis, f_cells,
-    vel_t, disp_t, wet_t, work, work_t, state_v, adjoint_v, mate_v, first_v, last_v,
+    decay, f_vx, f_vy, f_disp, f_wet, f_conc, f_cot, f_emis, f_cells,
+    vel_t, disp_t, wet_t, work, work_t, adjoint_v, mate_v, first_v, last_v,
     onehot, rows_v, cols_v, owner_v,
     y_send, y_recv, x_send, x_recv, xb_send, xb_recv, yb_send, yb_recv, ends_a, ends_b,
-    z_send, z_recv, p_send, p_recv, g_send, g_recv, total, grad_v,
-    in_sem, out_sem, mate_ssem, mate_rsem, ssem, rsem,
+    z_send, z_recv, p_send, p_recv, g_send, g_recv, total,
+    in_sem, mate_ssem, mate_rsem, ssem, rsem,
 ):
     gx, gy, en = lax.axis_index("gx"), lax.axis_index("gy"), lax.axis_index("ens")
     half = nsrc // ne
@@ -181,6 +186,7 @@
             [
                 (vel_y, f_vy), (disp, f_disp), (wet_cells, f_wet), (cot.at[0], f_cot),
                 (vel_x, f_vx), (cells, f_cells), (emission, f_emis), (conc.at[0], f_conc),
+                (decay_in, decay),
             ]
         )
     ]
@@ -189,16 +195,20 @@
         return (gx, wrapped(gy + o, ny), en)
 
     def x_peer(o):
-        return (wrapped(gx + o, nx), gy, en)
+        return (gx ^ o, gy, en)
+
+    def mate_peer(o):
+        return (gx ^ o, gy, mate[2])
 
     barrier = pltpu.get_barrier_semaphore()
-    for o in farthest_first(ny):
-        pl.semaphore_signal(barrier, inc=1, device_id=line_peer(o), device_id_type=MESH)
-    for load in loads:
+    greeted = [line_peer(o) for o in farthest_first(ny)]
+    greeted += [peer(o) for o in plane_order(nx) for peer in (x_peer, mate_peer)] + [mate]
+    for load in loads[:5]:
         load.start()
-    for o in farthest_first(nx):
-        pl.semaphore_signal(barrier, inc=1, device_id=x_peer(o), device_id_type=MESH)
-    pl.semaphore_signal(barrier, inc=1, device_id=mate, device_id_type=MESH)
+    for peer in greeted:
+        pl.semaphore_signal(barrier, inc=1, device_id=peer, device_id_type=MESH)
+    for load in loads[5:]:
+        load.start()
 
     def to_line(send, recv, slot):
         for o in farthest_first(ny):
@@ -209,7 +219,7 @@
         recv[gy] = send[...]
 
     def to_x(send, recv, slot):
-        for o in farthest_first(nx):
+        for o in plane_order(nx):
             pltpu.make_async_remote_copy(
                 src_ref=send, dst_ref=recv.at[gx], send_sem=ssem.at[slot],
                 recv_sem=rsem.at[slot], device_id=x_peer(o), device_id_type=MESH,
@@ -217,8 +227,8 @@
         recv[gx] = send[...]
 
     def to_each_x(send, recv, slot):
-        for o in farthest_first(nx):
-            peer = wrapped(gx + o, nx)
+        for o in plane_order(nx):
+            peer = gx ^ o
             pltpu.make_async_remote_copy(
                 src_ref=send.at[peer], dst_ref=recv.at[gx], send_sem=ssem.at[slot],
                 recv_sem=rsem.at[slot], device_id=x_peer(o), device_id_type=MESH,
@@ -254,7 +264,7 @@
             value = jnp.where(tracer == t, decay[t], value)
         return 0.5 * value
 
-    for i in range(4):
+    for i in (8, 0, 1, 2, 3):
         loads[i].wait()
     wet_f = f_wet[...].astype(F32)
     for field, ref in ((f_vy[...], vel_t), (f_disp[...], disp_t), (wet_f, wet_t)):
@@ -367,7 +377,7 @@
     ends_a[0:8, :] = zero8
     ends_b[0:8, :] = zero8
 
-    pl.semaphore_wait(barrier, ny - 1 + nx - 1 + 1)
+    pl.semaphore_wait(barrier, len(greeted))
     to_line(y_send, y_recv, 0)
     to_x(x_send, x_recv, 1)
 
@@ -526,11 +536,9 @@
     arrived(xb_recv, nx - 1, 4)
     ends_a[8 : 8 + 8 * nx, :] = flux_of(xb_recv)
     put(
-        work,
+        adjoint_out,
         x_line.finish(x_adj, column(adjoint_v), own_x(ends_a, gx), -own_x(ends_a, gx + 1)),
     )
-    adjoint_store = pltpu.make_async_copy(work, adjoint_out, out_sem.at[0])
-    adjoint_store.start()
 
     arrived(yb_recv, ny - 1, 3)
     jump = pcr_apply(
@@ -540,9 +548,7 @@
     ends_b[8 : 8 + ny, :] = y_before * jump
     head, tail = ends_a[pl.ds(7 + gy, 1), :], -ends_b[pl.ds(8 + gy, 1), :]
     put(work_t, y_line.finish(y_fwd, fy_part, head, tail))
-    state_v[...] = jnp.transpose(work_t[...])
-    state_store = pltpu.make_async_copy(state_v, state_out, out_sem.at[1])
-    state_store.start()
+    state_out[...] = jnp.transpose(work_t[...])
 
     arrived(g_recv, ny - 1, 6)
     sums = summed(g_recv, 0, width, ny)
@@ -550,16 +556,14 @@
         for i in range(tiles):
             total[t : t + 1, i * LANES : (i + 1) * LANES] = sums[tiles * t + i : tiles * t + i + 1]
 
-    def span(start, size):
-        return grad_v.at[:, pl.ds(pl.multiple_of(start, LANES), size)]
-
-    here = en * half + gx * chunk
-    for o in farthest_first(nx):
+    here = grad_out.at[:, pl.ds(pl.multiple_of(en * half + gx * chunk, LANES), chunk)]
+    peers = [peer(o) for o in plane_order(nx) for peer in (x_peer, mate_peer)] + [mate]
+    for peer in peers:
         pltpu.make_async_remote_copy(
-            src_ref=total, dst_ref=span(here, chunk), send_sem=ssem.at[7], recv_sem=rsem.at[7],
-            device_id=x_peer(o), device_id_type=MESH,
+            src_ref=total, dst_ref=here, send_sem=ssem.at[7], recv_sem=rsem.at[7],
+            device_id=peer, device_id_type=MESH,
         ).start()
-    grad_v[:, pl.ds(pl.multiple_of(here, LANES), chunk)] = total[...]
+    grad_out[:, pl.ds(pl.multiple_of(en * half + gx * chunk, LANES), chunk)] = total[...]
 
     sent(y_recv, ny - 1, 0)
     sent(x_recv, nx - 1, 1)
@@ -569,22 +573,19 @@
     sent(p_recv, nx - 1, 5)
     sent(g_recv, ny - 1, 6)
     to_mate.wait_send()
-    adjoint_store.wait()
-    state_store.wait()
-
-    rest = span(0, (nx - 1) * chunk)
+
+    rest = grad_out.at[:, pl.ds(0, len(peers) * chunk)]
+    pltpu.make_async_copy(rest, rest, ssem.at[7]).wait()
     pltpu.make_async_copy(rest, rest, rsem.at[7]).wait()
-    own_half = span(en * half, half)
-    swap = pltpu.make_async_remote_copy(
-        src_ref=own_half, dst_ref=own_half, send_sem=mate_ssem.at[1], recv_sem=mate_rsem.at[1],
-        device_id=mate, device_id_type=MESH,
-    )
-    swap.start()
-    pltpu.make_async_copy(rest, rest, ssem.at[7]).wait()
-    swap.wait()
-    grad_store = pltpu.make_async_copy(grad_v, grad_out, out_sem.at[2])
-    grad_store.start()
-    grad_store.wait()
+
+
+def store(state, adjoint, gradient, state_out, adjoint_out, grad_out, sem):
+    moves = ((gradient, grad_out), (state, state_out), (adjoint, adjoint_out))
+    copies = [pltpu.make_async_copy(m[0], m[1], sem.at[i]) for i, m in enumerate(moves)]
+    for copy in copies:
+        copy.start()
+    for copy in copies:
+        copy.wait()
 
 
 def per_device(
@@ -593,6 +594,13 @@
 ):
     nsrc = source_cell.shape[0]
     chunk = nsrc // (nx * ne)
+    operands = [
+        pltpu.with_memory_space_constraint(x, pltpu.HBM)
+        for x in (
+            decay_rate, concentration, cotangent, vel_x, vel_y, dispersion, wet_cells, emission,
+            source_cell.reshape(nsrc // LANES, LANES),
+        )
+    ]
     width = TR * chunk // LANES
     square = pltpu.VMEM((CELLS, COLS), F32)
     block = pltpu.VMEM((ROWS, COLS), F32)
@@ -603,20 +611,21 @@
     index = vmem(nsrc // LANES, LANES, dtype=jnp.int32)
     ends = vmem(8 + 8 * max(nx, ny), LANES)
     scratch = [
-        block, block, block, vmem(ROWS, COLS, dtype=jnp.int32),
+        pltpu.SMEM((TR,), F32), block, block, block, vmem(ROWS, COLS, dtype=jnp.int32),
         vmem(TR, ROWS, COLS), vmem(TR, ROWS, COLS), vmem(TR, nsrc), index,
-        square, square, square, square, square, square, square, square, square, square,
+        square, square, square, square, square, square, square, square, square,
         vmem(COLS, nsrc, dtype=BF16), index, index, index,
         vmem(8, LANES), vmem(ny, 8, LANES), vmem(32, LANES), vmem(nx, 32, LANES),
         vmem(8, LANES), vmem(nx, 8, LANES), vmem(8, LANES), vmem(ny, 8, LANES), ends, ends,
         vmem(nx, 2 * width, LANES), vmem(nx, 2 * width, LANES),
         vmem(nx, 8 + width, LANES), vmem(nx, 8 + width, LANES),
-        vmem(width, LANES), vmem(ny, width, LANES), vmem(TR, chunk), vmem(TR, nsrc),
-        pltpu.SemaphoreType.DMA((8,)), pltpu.SemaphoreType.DMA((3,)),
-        pltpu.SemaphoreType.DMA((2,)), pltpu.SemaphoreType.DMA((2,)),
+        vmem(width, LANES), vmem(ny, width, LANES), vmem(TR, chunk),
+        pltpu.SemaphoreType.DMA((9,)),
+        pltpu.SemaphoreType.DMA((1,)), pltpu.SemaphoreType.DMA((1,)),
         pltpu.SemaphoreType.DMA((8,)), pltpu.SemaphoreType.DMA((8,)),
     ]
     hbm = pl.BlockSpec(memory_space=pl.ANY)
+    on_chip = pl.BlockSpec(memory_space=pltpu.VMEM)
     state, adjoint, gradient = pl.pallas_call(
         functools.partial(kernel, nx, ny, ne, nsrc),
         out_shape=(
@@ -624,22 +633,31 @@
             jax.ShapeDtypeStruct((CELLS, COLS), F32),
             jax.ShapeDtypeStruct(emission.shape, F32),
         ),
-        in_specs=[pl.BlockSpec(memory_space=pltpu.SMEM)] + [hbm] * 8,
-        out_specs=(hbm, hbm, hbm),
+        in_specs=[hbm] * 9,
+        out_specs=(on_chip, on_chip, on_chip),
         scratch_shapes=scratch,
         compiler_params=pltpu.CompilerParams(
             collective_id=0, has_side_effects=True, vmem_limit_bytes=VMEM_BYTES
         ),
         name="adi_step",
-    )(
-        decay_rate, concentration, cotangent, vel_x, vel_y, dispersion, wet_cells, emission,
-        source_cell.reshape(nsrc // LANES, LANES),
-    )
+    )(*operands)
     shape = concentration.shape
-    return (state.reshape(shape), adjoint.reshape(shape), gradient)
-
-
-VMEM_BYTES = 60 * 1024 * 1024
+    return pl.pallas_call(
+        store,
+        out_shape=(
+            jax.ShapeDtypeStruct(shape, F32),
+            jax.ShapeDtypeStruct(shape, F32),
+            jax.ShapeDtypeStruct(emission.shape, F32),
+        ),
+        in_specs=[on_chip] * 3,
+        out_specs=(hbm, hbm, hbm),
+        scratch_shapes=[pltpu.SemaphoreType.DMA((3,))],
+        compiler_params=pltpu.CompilerParams(vmem_limit_bytes=VMEM_BYTES),
+        name="store",
+    )(state.reshape(shape), adjoint.reshape(shape), gradient)
+
+
+VMEM_BYTES = 32 * 1024 * 1024
 
 
 def solution(mesh):

time: 50.1 us -> 44.8 us (0.89)
  local copies, waits for them, and re-layouts: 2.8 us -> 0 us
  Pallas kernels: 46.4 us -> 44 us
    pallas_call x1, Pallas kernels: 46.4 us -> 43.3 us  [per_device(): pl.pallas_call(functools.partial(kernel, nx, ny, ne, nsrc), out_shape=(ja...]
    unnamed x7 -> x0, local copies, waits for them, and re-layouts: 2.8 us -> none
    pallas_call x0 -> x1, Pallas kernels: none -> 0.72 us  [per_device(): pl.pallas_call(store, out_shape=(jax.ShapeDtypeStruct(shape, F32), jax.Sh...]
where the time goes in v3:
time: 44.8 us; the launch traced here: 44.6 us
  Pallas kernels  44 us (98%)
  between operations  0.64 us (1%)
    pallas_call x1, Pallas kernels, per_device(): pl.pallas_call(functools.partial(kernel, nx, ny, ne, nsrc), out_shape=(ja...  43.3 us

profile of v3, /device:TPU:1, one launch (start us, length us, event | category | flops | bytes accessed | tf_op | source)
XLA Modules:
  0.0 44.6 jit_solution(14332867940977518365)
XLA Ops:
  0.6 43.3 %adi_step.1 = (f32[128,128]{1,0:T(8,128)S(1)}, f32[128,128]{1,0:T(8,128)S(1)}, f32[4,8192]{1,0:T(4,128)S(1)}) custom-call(f32[4]{0:T(128)} %decay_in.1, f32[1,4,32,128]{3,2,1,0:T(8,128)} %conc.1, f32[1,4,32,128]{3,2,1,0:T(8,128)} %cot.1, f32[32,128]{1,0:T(8,128)} %vel_x.1, f32[32,128]{1,0:T(8,128)} %vel_y.1, f32[32,128]{1,0:T(8,128)} %disp.1, ...), custom_call_target="tpu_custom_call" | custom-call | tf_op jit(solution)/shard_map/adi_step/pallas_call | solution.py:629
  43.9 0.7 %store.1 = (f32[1,4,32,128]{3,2,1,0:T(8,128)}, f32[1,4,32,128]{3,2,1,0:T(8,128)}, f32[4,8192]{1,0:T(4,128)}) custom-call(f32[1,4,32,128]{3,2,1,0:T(8,128)S(1)} %bitcast.3, f32[1,4,32,128]{3,2,1,0:T(8,128)S(1)} %bitcast.4, f32[4,8192]{1,0:T(4,128)S(1)} %get-tuple-element.8.gradient), custom_call_target="tpu_custom_call" | custom-call | tf_op jit(solution)/shard_map/store/pallas_call | solution.py:645

commit v4 on v3

--- a/solution.py
+++ b/solution.py
@@ -179,6 +179,7 @@
     tiles = chunk // LANES
     half_tiles = half // LANES
     mate = (gx, gy, wrapped(en + 1, ne))
+    assert tiles == 2
 
     loads = [
         pltpu.make_async_copy(src, dst, in_sem.at[i])
@@ -385,30 +386,46 @@
         high = values.astype(BF16)
         return jnp.concatenate([high, (values - high.astype(F32)).astype(BF16)], axis=1)
 
-    def pick(fields, send, at):
+    sub = lax.broadcasted_iota(jnp.int32, (8, LANES), 0)
+
+    def folded(parts):
+        for bit in (1, 2, 4):
+            keep = (sub & bit) == 0
+            parts = [
+                jnp.where(keep, a, b) + pltpu.roll(jnp.where(keep, b, a), bit, 0)
+                for a, b in zip(parts[0::2], parts[1::2])
+            ]
+        return parts[0]
+
+    def pick(fields, send, at, unrolled):
         left = jnp.concatenate([split_bf16(field) for field in fields], axis=0)
-        per_step = max(TILES, tiles)
+        per_step = min(TILES, half_tiles)
 
         def go(step, _):
             base = pl.multiple_of(en * half_tiles + step * per_step, per_step)
             row_tile = rows_v[pl.ds(base, per_step), :]
             hot = onehot[:, lanes(base, per_step)]
             found = jnp.dot(left, jnp.concatenate([hot, hot], axis=0), preferred_element_type=F32)
-            for i in range(per_step):
-                mask = row_iota == row_tile[i : i + 1, :]
-                block = step * (per_step // tiles) + i // tiles
+            masks = [row_iota == row_tile[i : i + 1, :] for i in range(per_step)]
+            for pair in range(per_step // 2):
                 for k, first in enumerate(at):
+                    parts = []
                     for t in range(TR):
-                        start = (k * TR + t) * ROWS
-                        line = found[start : start + ROWS, i * LANES : (i + 1) * LANES]
-                        line = jnp.sum(jnp.where(mask, line, 0.0), axis=0, keepdims=True)
-                        spot = first + tiles * t + i % tiles
-                        send[block, spot : spot + 1, :] = line
+                        for i in (2 * pair, 2 * pair + 1):
+                            start = (k * TR + t) * ROWS
+                            line = found[start : start + ROWS, i * LANES : (i + 1) * LANES]
+                            line = jnp.where(masks[i], line, 0.0)
+                            parts.append((line[0:8] + line[8:16]) + (line[16:24] + line[24:32]))
+                    send[step * (per_step // 2) + pair, first : first + 8, :] = folded(parts)
             return 0
 
-        lax.fori_loop(0, half_tiles // per_step, go, 0)
-
-    pick((first_v[...], last_v[...]), z_send, (0, TR * tiles))
+        if unrolled:
+            for step in range(half_tiles // per_step):
+                go(step, 0)
+        else:
+            lax.fori_loop(0, half_tiles // per_step, go, 0)
+
+    pick((first_v[...], last_v[...]), z_send, (0, TR * tiles), False)
     to_each_x(z_send, z_recv, 2)
 
     def x_piece(ref, k):
@@ -492,7 +509,7 @@
     both_edges = x_line.edges([strided(work, q) if q in (0, e) else None for q in range(Q)])
     for d in range(nx):
         p_send[d, 0:8, :] = both_edges
-    pick((both,), p_send, (8,))
+    pick((both,), p_send, (8,), True)
     to_each_x(p_send, p_recv, 5)
 
     y_fwd_factors = pcr_factor(y_below, y_center, y_above, ny, 1)

time: 44.8 us -> 44.4 us (level)
  no operation moved by 1% of the time
where the time goes in v4:
time: 44.4 us; the launch traced here: 44.3 us
  Pallas kernels  43.6 us (98%)
  between operations  0.64 us (1%)
    pallas_call x1, Pallas kernels, per_device(): pl.pallas_call(functools.partial(kernel, nx, ny, ne, nsrc), out_shape=(ja...  42.9 us

profile of v4, /device:TPU:1, one launch (start us, length us, event | category | flops | bytes accessed | tf_op | source)
XLA Modules:
  0.0 44.3 jit_solution(2885540685381355992)
XLA Ops:
  0.6 42.9 %adi_step.1 = (f32[128,128]{1,0:T(8,128)S(1)}, f32[128,128]{1,0:T(8,128)S(1)}, f32[4,8192]{1,0:T(4,128)S(1)}) custom-call(f32[4]{0:T(128)} %decay_in.1, f32[1,4,32,128]{3,2,1,0:T(8,128)} %conc.1, f32[1,4,32,128]{3,2,1,0:T(8,128)} %cot.1, f32[32,128]{1,0:T(8,128)} %vel_x.1, f32[32,128]{1,0:T(8,128)} %vel_y.1, f32[32,128]{1,0:T(8,128)} %disp.1, ...), custom_call_target="tpu_custom_call" | custom-call | tf_op jit(solution)/shard_map/adi_step/pallas_call | solution.py:646
  43.6 0.7 %store.1 = (f32[1,4,32,128]{3,2,1,0:T(8,128)}, f32[1,4,32,128]{3,2,1,0:T(8,128)}, f32[4,8192]{1,0:T(4,128)}) custom-call(f32[1,4,32,128]{3,2,1,0:T(8,128)S(1)} %bitcast.3, f32[1,4,32,128]{3,2,1,0:T(8,128)S(1)} %bitcast.4, f32[4,8192]{1,0:T(4,128)S(1)} %get-tuple-element.8.gradient), custom_call_target="tpu_custom_call" | custom-call | tf_op jit(solution)/shard_map/store/pallas_call | solution.py:662

commit v5 on v4

--- a/solution.py
+++ b/solution.py
@@ -447,31 +447,6 @@
         block = ref[pl.ds(pl.multiple_of(8 * at, 8), 8), :]
         return jnp.where(x_line.last, block, rolled(block, -1))
 
-    arrived(x_recv, nx - 1, 1)
-    index = lax.broadcasted_iota(jnp.int32, (nx, LANES), 0)
-    x_before, x_after = (
-        expanded(face) for face in faces(*[single(x_recv, 24 + k, nx) for k in range(4)], index, nx)
-    )
-    diagonal, corner = x_piece(x_recv, 1), x_piece(x_recv, 2)
-    x_below = -corner * rolled(x_after, 8)
-    x_center = 1.0 + diagonal * x_before + from_next(diagonal) * x_after
-    block_index = lax.broadcasted_iota(jnp.int32, (8 * nx, LANES), 0) // 8
-    x_above = jnp.where(
-        block_index == nx - 1, 0.0, -from_next(corner) * rolled(x_before, -8)
-    )
-    terms = x_piece(x_recv, 0)
-    jump = pcr_apply(pcr_factor(x_below, x_center, x_above, nx, 8), terms - from_next(terms))
-    ends_a[8 : 8 + 8 * nx, :] = x_after * jump
-    ends_b[8 : 8 + 8 * nx, :] = x_before * jump
-    put(work, x_line.finish(x_fwd, fx_part, own_x(ends_a, gx), -own_x(ends_b, gx + 1)))
-    work_t[...] = jnp.transpose(work[...])
-    fy_part = y_line.solve(y_fwd, column(work_t))
-    yb_send[0:1, :] = fy_part[0][0:1]
-    yb_send[1:2, :] = fy_part[e][7:8]
-    yb_send[2:8, :] = zero8[0:6]
-    to_line(yb_send, yb_recv, 3)
-    x_factors = pcr_factor(rolled(x_above, 8), x_center, rolled(x_below, -8), nx, 8)
-
     arrived(y_recv, ny - 1, 0)
     raw = single(y_recv, 6, ny)
     tracer_n = jnp.broadcast_to(tracer_row, (ny, LANES))
@@ -501,7 +476,6 @@
     )
     to_mate.start()
     xb_send[...] = x_line.edges(ax_part)
-    to_x(xb_send, xb_recv, 4)
 
     to_mate.wait_recv()
     both = adjoint_v[...] + mate_v[...]
@@ -511,6 +485,32 @@
         p_send[d, 0:8, :] = both_edges
     pick((both,), p_send, (8,), True)
     to_each_x(p_send, p_recv, 5)
+    to_x(xb_send, xb_recv, 4)
+
+    arrived(x_recv, nx - 1, 1)
+    index = lax.broadcasted_iota(jnp.int32, (nx, LANES), 0)
+    x_before, x_after = (
+        expanded(face) for face in faces(*[single(x_recv, 24 + k, nx) for k in range(4)], index, nx)
+    )
+    diagonal, corner = x_piece(x_recv, 1), x_piece(x_recv, 2)
+    x_below = -corner * rolled(x_after, 8)
+    x_center = 1.0 + diagonal * x_before + from_next(diagonal) * x_after
+    block_index = lax.broadcasted_iota(jnp.int32, (8 * nx, LANES), 0) // 8
+    x_above = jnp.where(
+        block_index == nx - 1, 0.0, -from_next(corner) * rolled(x_before, -8)
+    )
+    terms = x_piece(x_recv, 0)
+    jump = pcr_apply(pcr_factor(x_below, x_center, x_above, nx, 8), terms - from_next(terms))
+    ends_a[8 : 8 + 8 * nx, :] = x_after * jump
+    ends_b[8 : 8 + 8 * nx, :] = x_before * jump
+    put(work, x_line.finish(x_fwd, fx_part, own_x(ends_a, gx), -own_x(ends_b, gx + 1)))
+    work_t[...] = jnp.transpose(work[...])
+    fy_part = y_line.solve(y_fwd, column(work_t))
+    yb_send[0:1, :] = fy_part[0][0:1]
+    yb_send[1:2, :] = fy_part[e][7:8]
+    yb_send[2:8, :] = zero8[0:6]
+    to_line(yb_send, yb_recv, 3)
+    x_factors = pcr_factor(rolled(x_above, 8), x_center, rolled(x_below, -8), nx, 8)
 
     y_fwd_factors = pcr_factor(y_below, y_center, y_above, ny, 1)
     arrived(z_recv, nx - 1, 2)

time: 44.4 us -> 44.2 us (level)
  no operation moved by 1% of the time
where the time goes in v5:
time: 44.2 us; the launch traced here: 44.1 us
  Pallas kernels  43.4 us (98%)
  between operations  0.64 us (1%)
    pallas_call x1, Pallas kernels, per_device(): pl.pallas_call(functools.partial(kernel, nx, ny, ne, nsrc), out_shape=(ja...  42.7 us

profile of v5, /device:TPU:1, one launch (start us, length us, event | category | flops | bytes accessed | tf_op | source)
XLA Modules:
  0.0 44.1 jit_solution(8981680897120069305)
XLA Ops:
  0.6 42.7 %adi_step.1 = (f32[128,128]{1,0:T(8,128)S(1)}, f32[128,128]{1,0:T(8,128)S(1)}, f32[4,8192]{1,0:T(4,128)S(1)}) custom-call(f32[4]{0:T(128)} %decay_in.1, f32[1,4,32,128]{3,2,1,0:T(8,128)} %conc.1, f32[1,4,32,128]{3,2,1,0:T(8,128)} %cot.1, f32[32,128]{1,0:T(8,128)} %vel_x.1, f32[32,128]{1,0:T(8,128)} %vel_y.1, f32[32,128]{1,0:T(8,128)} %disp.1, ...), custom_call_target="tpu_custom_call" | custom-call | tf_op jit(solution)/shard_map/adi_step/pallas_call | solution.py:646
  43.3 0.7 %store.1 = (f32[1,4,32,128]{3,2,1,0:T(8,128)}, f32[1,4,32,128]{3,2,1,0:T(8,128)}, f32[4,8192]{1,0:T(4,128)}) custom-call(f32[1,4,32,128]{3,2,1,0:T(8,128)S(1)} %bitcast.3, f32[1,4,32,128]{3,2,1,0:T(8,128)S(1)} %bitcast.4, f32[4,8192]{1,0:T(4,128)S(1)} %get-tuple-element.8.gradient), custom_call_target="tpu_custom_call" | custom-call | tf_op jit(solution)/shard_map/store/pallas_call | solution.py:662

commit v6 on v5

--- a/solution.py
+++ b/solution.py
@@ -170,7 +170,7 @@
     vel_t, disp_t, wet_t, work, work_t, adjoint_v, mate_v, first_v, last_v,
     onehot, rows_v, cols_v, owner_v,
     y_send, y_recv, x_send, x_recv, xb_send, xb_recv, yb_send, yb_recv, ends_a, ends_b,
-    z_send, z_recv, p_send, p_recv, g_send, g_recv, total,
+    z_send, z_recv, e_send, e_recv, p_send, p_recv, g_send, g_recv, total,
     in_sem, mate_ssem, mate_rsem, ssem, rsem,
 ):
     gx, gy, en = lax.axis_index("gx"), lax.axis_index("gy"), lax.axis_index("ens")
@@ -204,10 +204,11 @@
     barrier = pltpu.get_barrier_semaphore()
     greeted = [line_peer(o) for o in farthest_first(ny)]
     greeted += [peer(o) for o in plane_order(nx) for peer in (x_peer, mate_peer)] + [mate]
-    for load in loads[:5]:
-        load.start()
-    for peer in greeted:
+    for i, peer in enumerate(greeted):
         pl.semaphore_signal(barrier, inc=1, device_id=peer, device_id_type=MESH)
+        if i == 2:
+            for load in loads[:5]:
+                load.start()
     for load in loads[5:]:
         load.start()
 
@@ -481,9 +482,9 @@
     both = adjoint_v[...] + mate_v[...]
     work[...] = both
     both_edges = x_line.edges([strided(work, q) if q in (0, e) else None for q in range(Q)])
-    for d in range(nx):
-        p_send[d, 0:8, :] = both_edges
-    pick((both,), p_send, (8,), True)
+    e_send[...] = both_edges
+    to_x(e_send, e_recv, 8)
+    pick((both,), p_send, (0,), True)
     to_each_x(p_send, p_recv, 5)
     to_x(xb_send, xb_recv, 4)
 
@@ -524,13 +525,13 @@
     width = TR * tiles
     z_first, z_last = summed(z_recv, 0, width, nx), summed(z_recv, width, width, nx)
 
-    arrived(p_recv, nx - 1, 5)
+    arrived(e_recv, nx - 1, 8)
 
     def flux_of(ref):
         terms = x_piece(ref, 0)
         return pcr_apply(x_factors, x_before * terms - x_after * from_next(terms))
 
-    flux = flux_of(p_recv)
+    flux = flux_of(e_recv)
     mine = pl.multiple_of(en * half_tiles + gx * tiles, tiles)
     hot = onehot[:, lanes(mine, tiles)]
     found = jnp.dot(
@@ -547,7 +548,8 @@
             spot = slice(tiles * t + i, tiles * t + i + 1)
             at = slice(2 * t + 1, 2 * t + 2)
             g_send[spot, :] = z_first[spot] * into[at] - z_last[spot] * out[at]
-    g_send[...] = g_send[...] + summed(p_recv, 8, width, nx)
+    arrived(p_recv, nx - 1, 5)
+    g_send[...] = g_send[...] + summed(p_recv, 0, width, nx)
     to_line(g_send, g_recv, 6)
 
     arrived(xb_recv, nx - 1, 4)
@@ -588,6 +590,7 @@
     sent(yb_recv, ny - 1, 3)
     sent(xb_recv, nx - 1, 4)
     sent(p_recv, nx - 1, 5)
+    sent(e_recv, nx - 1, 8)
     sent(g_recv, ny - 1, 6)
     to_mate.wait_send()
 
@@ -635,11 +638,11 @@
         vmem(8, LANES), vmem(ny, 8, LANES), vmem(32, LANES), vmem(nx, 32, LANES),
         vmem(8, LANES), vmem(nx, 8, LANES), vmem(8, LANES), vmem(ny, 8, LANES), ends, ends,
         vmem(nx, 2 * width, LANES), vmem(nx, 2 * width, LANES),
-        vmem(nx, 8 + width, LANES), vmem(nx, 8 + width, LANES),
+        vmem(8, LANES), vmem(nx, 8, LANES), vmem(nx, width, LANES), vmem(nx, width, LANES),
         vmem(width, LANES), vmem(ny, width, LANES), vmem(TR, chunk),
         pltpu.SemaphoreType.DMA((9,)),
         pltpu.SemaphoreType.DMA((1,)), pltpu.SemaphoreType.DMA((1,)),
-        pltpu.SemaphoreType.DMA((8,)), pltpu.SemaphoreType.DMA((8,)),
+        pltpu.SemaphoreType.DMA((9,)), pltpu.SemaphoreType.DMA((9,)),
     ]
     hbm = pl.BlockSpec(memory_space=pl.ANY)
     on_chip = pl.BlockSpec(memory_space=pltpu.VMEM)

time: 44.2 us -> 43.7 us (0.989)
  Pallas kernels: 43.4 us -> 42.9 us
    pallas_call x1, Pallas kernels: 42.7 us -> 42.2 us  [per_device(): pl.pallas_call(functools.partial(kernel, nx, ny, ne, nsrc), out_shape=(ja...]
where the time goes in v6:
time: 43.7 us; the launch traced here: 43.5 us
  Pallas kernels  42.9 us (98%)
  between operations  0.64 us (1%)
    pallas_call x1, Pallas kernels, per_device(): pl.pallas_call(functools.partial(kernel, nx, ny, ne, nsrc), out_shape=(ja...  42.2 us

profile of v6, /device:TPU:1, one launch (start us, length us, event | category | flops | bytes accessed | tf_op | source)
XLA Modules:
  0.0 43.5 jit_solution(1346502215264729428)
XLA Ops:
  0.6 42.2 %adi_step.1 = (f32[128,128]{1,0:T(8,128)S(1)}, f32[128,128]{1,0:T(8,128)S(1)}, f32[4,8192]{1,0:T(4,128)S(1)}) custom-call(f32[4]{0:T(128)} %decay_in.1, f32[1,4,32,128]{3,2,1,0:T(8,128)} %conc.1, f32[1,4,32,128]{3,2,1,0:T(8,128)} %cot.1, f32[32,128]{1,0:T(8,128)} %vel_x.1, f32[32,128]{1,0:T(8,128)} %vel_y.1, f32[32,128]{1,0:T(8,128)} %disp.1, ...), custom_call_target="tpu_custom_call" | custom-call | tf_op jit(solution)/shard_map/adi_step/pallas_call | solution.py:649
  42.8 0.7 %store.1 = (f32[1,4,32,128]{3,2,1,0:T(8,128)}, f32[1,4,32,128]{3,2,1,0:T(8,128)}, f32[4,8192]{1,0:T(4,128)}) custom-call(f32[1,4,32,128]{3,2,1,0:T(8,128)S(1)} %bitcast.3, f32[1,4,32,128]{3,2,1,0:T(8,128)S(1)} %bitcast.4, f32[4,8192]{1,0:T(4,128)S(1)} %get-tuple-element.8.gradient), custom_call_target="tpu_custom_call" | custom-call | tf_op jit(solution)/shard_map/store/pallas_call | solution.py:665

commit v7 on v6

--- a/solution.py
+++ b/solution.py
@@ -421,8 +421,21 @@
             return 0
 
         if unrolled:
-            for step in range(half_tiles // per_step):
-                go(step, 0)
+            steps, blocks = half_tiles // per_step, per_step // tiles
+            order = plane_order(steps) + [0]
+            middle = steps // 2
+            for group in (order[:middle], order[middle:]):
+                for far in group:
+                    go((gx // blocks) ^ far, 0)
+                for near in plane_order(blocks) + [0]:
+                    for o in [far * blocks + near for far in group]:
+                        if o:
+                            pltpu.make_async_remote_copy(
+                                src_ref=p_send.at[gx ^ o], dst_ref=p_recv.at[gx],
+                                send_sem=ssem.at[5], recv_sem=rsem.at[5],
+                                device_id=x_peer(o), device_id_type=MESH,
+                            ).start()
+            p_recv[gx] = p_send[gx]
         else:
             lax.fori_loop(0, half_tiles // per_step, go, 0)
 
@@ -485,7 +498,6 @@
     e_send[...] = both_edges
     to_x(e_send, e_recv, 8)
     pick((both,), p_send, (0,), True)
-    to_each_x(p_send, p_recv, 5)
     to_x(xb_send, xb_recv, 4)
 
     arrived(x_recv, nx - 1, 1)

time: 43.7 us -> 43.7 us (level)
  no operation moved by 1% of the time
where the time goes in v7:
time: 43.7 us; the launch traced here: 43.6 us
  Pallas kernels  42.9 us (98%)
  between operations  0.64 us (1%)
    pallas_call x1, Pallas kernels, per_device(): pl.pallas_call(functools.partial(kernel, nx, ny, ne, nsrc), out_shape=(ja...  42.2 us

profile of v7, /device:TPU:1, one launch (start us, length us, event | category | flops | bytes accessed | tf_op | source)
XLA Modules:
  0.0 43.6 jit_solution(17761602625916504828)
XLA Ops:
  0.6 42.2 %adi_step.1 = (f32[128,128]{1,0:T(8,128)S(1)}, f32[128,128]{1,0:T(8,128)S(1)}, f32[4,8192]{1,0:T(4,128)S(1)}) custom-call(f32[4]{0:T(128)} %decay_in.1, f32[1,4,32,128]{3,2,1,0:T(8,128)} %conc.1, f32[1,4,32,128]{3,2,1,0:T(8,128)} %cot.1, f32[32,128]{1,0:T(8,128)} %vel_x.1, f32[32,128]{1,0:T(8,128)} %vel_y.1, f32[32,128]{1,0:T(8,128)} %disp.1, ...), custom_call_target="tpu_custom_call" | custom-call | tf_op jit(solution)/shard_map/adi_step/pallas_call | solution.py:661
  42.8 0.7 %store.1 = (f32[1,4,32,128]{3,2,1,0:T(8,128)}, f32[1,4,32,128]{3,2,1,0:T(8,128)}, f32[4,8192]{1,0:T(4,128)}) custom-call(f32[1,4,32,128]{3,2,1,0:T(8,128)S(1)} %bitcast.3, f32[1,4,32,128]{3,2,1,0:T(8,128)S(1)} %bitcast.4, f32[4,8192]{1,0:T(4,128)S(1)} %get-tuple-element.8.gradient), custom_call_target="tpu_custom_call" | custom-call | tf_op jit(solution)/shard_map/store/pallas_call | solution.py:677

commit v8 on v7

--- a/solution.py
+++ b/solution.py
@@ -492,11 +492,10 @@
     xb_send[...] = x_line.edges(ax_part)
 
     to_mate.wait_recv()
+    first_sum, last_sum = (strided(adjoint_v, q) + strided(mate_v, q) for q in (0, e))
+    e_send[...] = jnp.where(x_line.last, last_sum, first_sum)
+    to_x(e_send, e_recv, 8)
     both = adjoint_v[...] + mate_v[...]
-    work[...] = both
-    both_edges = x_line.edges([strided(work, q) if q in (0, e) else None for q in range(Q)])
-    e_send[...] = both_edges
-    to_x(e_send, e_recv, 8)
     pick((both,), p_send, (0,), True)
     to_x(xb_send, xb_recv, 4)
 

time: 43.7 us -> 43.7 us (level)
  no operation moved by 1% of the time
where the time goes in v8:
time: 43.7 us; the launch traced here: 43.6 us
  Pallas kernels  42.9 us (98%)
  between operations  0.64 us (1%)
    pallas_call x1, Pallas kernels, per_device(): pl.pallas_call(functools.partial(kernel, nx, ny, ne, nsrc), out_shape=(ja...  42.2 us

profile of v8, /device:TPU:1, one launch (start us, length us, event | category | flops | bytes accessed | tf_op | source)
XLA Modules:
  0.0 43.6 jit_solution(4974657563752697376)
XLA Ops:
  0.6 42.2 %adi_step.1 = (f32[128,128]{1,0:T(8,128)S(1)}, f32[128,128]{1,0:T(8,128)S(1)}, f32[4,8192]{1,0:T(4,128)S(1)}) custom-call(f32[4]{0:T(128)} %decay_in.1, f32[1,4,32,128]{3,2,1,0:T(8,128)} %conc.1, f32[1,4,32,128]{3,2,1,0:T(8,128)} %cot.1, f32[32,128]{1,0:T(8,128)} %vel_x.1, f32[32,128]{1,0:T(8,128)} %vel_y.1, f32[32,128]{1,0:T(8,128)} %disp.1, ...), custom_call_target="tpu_custom_call" | custom-call | tf_op jit(solution)/shard_map/adi_step/pallas_call | solution.py:660
  42.8 0.7 %store.1 = (f32[1,4,32,128]{3,2,1,0:T(8,128)}, f32[1,4,32,128]{3,2,1,0:T(8,128)}, f32[4,8192]{1,0:T(4,128)}) custom-call(f32[1,4,32,128]{3,2,1,0:T(8,128)S(1)} %bitcast.3, f32[1,4,32,128]{3,2,1,0:T(8,128)S(1)} %bitcast.4, f32[4,8192]{1,0:T(4,128)S(1)} %get-tuple-element.8.gradient), custom_call_target="tpu_custom_call" | custom-call | tf_op jit(solution)/shard_map/store/pallas_call | solution.py:676
